TPU v7x, 512 devices: a whole 4x8x8 slice. The times are simulated.
512 devices in a mesh: freq: 4 (over x), row: 8 (over z), col: 16 (over y, core).
Axes of the slice: x: 4, y: 8, z: 8, core: 2. Of those that a mesh axis runs over, the one named last changes fastest.
Arguments:
- traces: bfloat16 [2048, 2048, 128], P(('freq', 'row', 'col')), may hold values from -6 to 6
- source_inverse: float32 [2, 16], replicated, may hold values from 0.5 to 1.5
Outputs:
- multiples: bfloat16 [2048, 2048, 128], P(('freq', 'row', 'col'))
All inputs are finite; a program needn't handle non-finite values.
Results may differ from a plain program's by a relative error of at most 0.0084.
Values may be sent and summed in bfloat16 or wider, within the bound.
A program may use at most 64 MiB of HBM per device.

v0:
```python
import math

import jax
import jax.numpy as jnp
from jax import lax
from jax.sharding import PartitionSpec as P


def dft_tables(count, length):
    bins = jnp.arange(count, dtype=jnp.int32) + 1
    times = jnp.arange(length, dtype=jnp.int32)
    index = bins[:, None] * times[None, :] % length
    angle = index.astype(jnp.float32) * (2.0 * math.pi / length)
    cosine = jnp.cos(angle)
    sine = jnp.sin(angle)
    norm = 1.0 / math.sqrt(length)
    stacked = jnp.concatenate([cosine, -sine], 0)
    forward = (stacked * norm).astype(jnp.bfloat16)
    inverse = (stacked * (2.0 * norm)).astype(jnp.bfloat16)
    return (forward, inverse)


def complex_block(left, right):
    parts = jnp.einsum("pjik,qjkl->pqjil", left, right, preferred_element_type=jnp.float32)
    return jnp.stack([parts[0, 0] - parts[1, 1], parts[0, 1] + parts[1, 0]])


def on_device(traces, source_inverse):
    groups = lax.axis_size("freq")
    rows = lax.axis_size("row")
    cols = lax.axis_size("col")
    shots = traces.shape[0]
    width = traces.shape[1]
    length = traces.shape[2]
    count = source_inverse.shape[1]
    band = count // groups
    block = width // cols
    panel_rows = cols * groups * shots
    forward, inverse = dft_tables(count, length)
    pieces = traces.reshape(shots, cols, block, length)
    table = forward.reshape(2, groups, band, length)
    spectra = jnp.einsum(
        "scbt,pgjt->gcpjsb", pieces, table, preferred_element_type=jnp.float32
    ).astype(jnp.bfloat16)
    spectra = spectra.reshape(groups * cols, 2, band, shots, block)
    arrived = lax.all_to_all(spectra, ("freq", "col"), split_axis=0, concat_axis=0, tiled=True)
    arrived = arrived.reshape(groups, cols, 2, band, shots, block)
    local_block = jnp.transpose(arrived, (2, 3, 1, 0, 4, 5)).reshape(2, band, panel_rows, block)
    column_panel = lax.all_gather(local_block, "row", axis=2, tiled=True)
    column_panel = column_panel.reshape(2, band, rows, cols, groups, shots, block)
    column_panel = jnp.transpose(column_panel, (0, 1, 4, 2, 3, 5, 6)).reshape(2, band, width, block)
    product = complex_block(lax.all_gather(local_block, "col", axis=3, tiled=True), column_panel)
    group = lax.axis_index("freq")
    weights = lax.dynamic_slice_in_dim(source_inverse, group * band, band, 1)
    w_real = weights[0][:, None, None]
    w_imag = weights[1][:, None, None]
    scale = 1.0 / math.sqrt(width)
    pred_real = (w_real * product[0] - w_imag * product[1]) * scale
    pred_imag = (w_real * product[1] + w_imag * product[0]) * scale
    predicted = jnp.stack([pred_real, pred_imag]).astype(jnp.bfloat16)
    predicted = predicted.reshape(2, band, cols, groups, shots, block)
    outgoing = jnp.transpose(predicted, (3, 2, 0, 1, 4, 5)).reshape(
        groups * cols, 2, band, shots, block
    )
    returned = lax.all_to_all(outgoing, ("freq", "col"), split_axis=0, concat_axis=0, tiled=True)
    returned = returned.reshape(groups, cols, 2, band, shots, block)
    inverse_table = inverse.reshape(2, groups, band, length)
    result = jnp.einsum(
        "gcpjsb,pgjt->scbt", returned, inverse_table, preferred_element_type=jnp.float32
    )
    return result.reshape(shots, width, length).astype(jnp.bfloat16)


def solution(mesh):
    in_specs = (P(("freq", "row", "col"), None, None), P())
    out_specs = P(("freq", "row", "col"), None, None)
    return jax.shard_map(
        on_device, mesh=mesh, in_specs=in_specs, out_specs=out_specs, check_vma=False
    )
```

profile of v0, /device:TPU:1, one launch (start us, length us, event | category | flops | bytes accessed | tf_op | source)
XLA Modules:
  0.0 210.3 jit_solution(11768684624941488458)
XLA Ops:
  6.5 0.0 copy-start
  6.5 0.0 all-gather.3.cloned.1.call-start
  6.5 0.1 fusion.18
  6.7 1.4 copy-done
  8.1 0.0 copy-start.1
  8.1 0.8 fusion.9
  8.9 0.1 copy.14
  9.0 0.4 copy.15
  9.5 28.7 %all_to_all.10 = bf16[64,2,4,4,128]{4,3,2,1,0:T(4,128)(2,1)S(1)} all-to-all(bf16[64,2,4,4,128]{4,3,2,1,0:T(4,128)(2,1)S(1)} %copy.15), channel_id=1, replica_groups=mesh['freq'=4,'row'=8,'col'=16] {'freq','col'}, dimensions={0} | all-to-all | bytes 1048576 | tf_op jit(solution)/shard_map/all_to_all | solution.py:46
  38.2 0.2 copy.16
  38.4 1.2 copy.17
  39.6 0.0 all-gather.3.cloned.1.call-update
  39.6 0.0 all-gather.5.cloned.1.call-start
  39.7 0.7 all-gather.5.cloned.1.call-update
  40.4 0.0 copy-done.1
  40.4 0.1 constant_dynamic-slice_fusion
  40.5 57.7 %all-gather.3.cloned.1.call-done = bf16[2,4,2048,128]{3,2,0,1:T(8,128)(2,1)} async-done(((bf16[2,4,256,128]{3,2,0,1:T(8,128)(2,1)}), bf16[2,4,2048,128]{3,2,0,1:T(8,128)(2,1)}) %all-gather.3.cloned.1.call-update) | async-done | bytes 4194320 | tf_op jit(solution)/shard_map/all_gather | solution.py:49
  98.2 6.5 %copy.18 = bf16[2,4,8,16,4,4,128]{6,5,3,2,4,1,0:T(4,128)(2,1)} copy(bf16[2,4,8,16,4,4,128]{6,5,4,3,2,0,1:T(4,128)(2,1)} %bitcast.60) | data formatting | bytes 8388608 | tf_op jit(solution)/shard_map/reshape | solution.py:50
  104.7 62.7 %all-gather.5.cloned.1.call-done = bf16[2,4,256,2048]{3,2,0,1:T(8,128)(2,1)} async-done(((bf16[2,4,256,128]{3,2,0,1:T(8,128)(2,1)}), bf16[2,4,256,2048]{3,2,0,1:T(8,128)(2,1)}) %all-gather.5.cloned.1.call-update) | async-done | bytes 8388624 | tf_op jit(solution)/shard_map/all_gather | solution.py:52
  167.4 7.3 %fusion.3 = f32[2,2,4,256,128]{3,4,0,1,2:T(8,128)S(1)} fusion(bf16[2,4,256,2048]{3,2,0,1:T(8,128)(2,1)} %all-gather.5.cloned.1.call-done, bf16[2,4,2048,128,1]{3,2,1,0,4:T(8,128)(2,1)} %bitcast.61), kind=kOutput, calls=%fused_computation.4 | convolution fusion | flops 2147483648 | bytes 14680064 | tf_op jit(solution)/shard_map/pjik,qjkl->pqjil/dot_general | solution.py:24
  174.7 1.0 slice_add_fusion
  175.7 0.2 copy.20
  175.9 1.2 copy.21
  177.1 0.4 multiply_convert_fusion.1
  177.5 0.4 maximum_bitcast_fusion
  177.9 0.1 copy.22
  178.1 0.4 copy.23
  178.5 22.5 %all_to_all.11 = bf16[64,2,4,4,128]{4,3,2,1,0:T(4,128)(2,1)S(1)} all-to-all(bf16[64,2,4,4,128]{4,3,2,1,0:T(4,128)(2,1)S(1)} %copy.23), channel_id=1, replica_groups=mesh['freq'=4,'row'=8,'col'=16] {'freq','col'}, dimensions={0} | all-to-all | bytes 1048576 | tf_op jit(solution)/shard_map/all_to_all | solution.py:65
  200.9 1.1 fusion.8
  202.0 1.5 copy.27
  (3 shorter events, 0.0 us)
Async XLA Ops:
  6.5 1.6 copy-start
  6.5 91.7 %all-gather.3.cloned.1.call-start = ((), (), s32[]{:S(2)}) async-start(), calls=%async_computation.2 | async-start | bytes 4718592 | tf_op jit(solution)/shard_map/all_gather | solution.py:49
  8.1 32.3 %copy-start.1 = (f32[2,16]{1,0:T(2,128)S(1)}, f32[2,16]{1,0:T(2,128)}, u32[]{:S(2)}) copy-start(f32[2,16]{1,0:T(2,128)} %param.3) | copy-start | bytes 388
  39.6 127.8 %all-gather.5.cloned.1.call-start = ((), (), s32[]{:S(2)}) async-start(), calls=%async_computation.3 | async-start | bytes 8912896 | tf_op jit(solution)/shard_map/all_gather | solution.py:52
Sparse Core Ops, SparseCore 0:
  39.8 58.3 all-gather.2
  100.2 67.1 all-gather.4
where the time goes:
time: 211 us; the launch traced here: 210 us
  waiting for transfers between devices  121 us (57%)
  blocking collectives  51.2 us (24%)
  between operations  13.5 us (6%)
  local copies, waits for them, and re-layouts  13.4 us (6%)
  matrix products  9.14 us (4%)
    all_gather x1, waiting for transfers between devices, on_device(): lax.all_gather(local_block, 'col', axis=3, tiled=True)  62.7 us
    all_gather x1, waiting for transfers between devices, on_device(): column_panel = lax.all_gather(local_block, 'row', axis=2, tiled=True)  57.7 us
    all_to_all x1, blocking collectives, on_device(): lax.all_to_all(spectra, ('freq', 'col'), split_axis=0, concat_axis=0, til...  28.7 us
    all_to_all x1, blocking collectives, on_device(): lax.all_to_all(outgoing, ('freq', 'col'), split_axis=0, concat_axis=0, ti...  22.5 us
    dot_general x1, matrix products, complex_block(): jnp.einsum('pjik,qjkl->pqjil', left, right, preferred_element_type=jnp.fl...  7.29 us
    reshape x1, local copies, waits for them, and re-layouts, on_device(): column_panel.reshape(2, band, rows, cols, groups, shots, block)  6.53 us
  transfers between devices with their start and end apart: 2, of which 2 were waited for; matrix products, arithmetic and copies ran while one was open for 3% of the time, Pallas kernels for 0%

commit v1 on v0

v1 whole, which is shorter than its diff:
```python
import functools
import math

import jax
import jax.numpy as jnp
import numpy as np
from jax import lax
from jax.experimental import pallas as pl
from jax.experimental.pallas import tpu as pltpu
from jax.sharding import PartitionSpec as P

MESH = pl.DeviceIdType.MESH
BF16 = jnp.bfloat16
F32 = jnp.float32
VMEM_LIMIT = 44 * 1024 * 1024


def tables(count, length):
    bins = np.arange(count, dtype=np.int32) + 1
    times = np.arange(length, dtype=np.int32)
    index = bins[:, None] * times[None, :] % length
    angle = index.astype(np.float32) * np.float32(2.0 * math.pi / length)
    norm = np.float32(1.0 / math.sqrt(length))
    stacked = np.stack([np.cos(angle), -np.sin(angle)])
    forward = np.zeros((count, 2, 4, 4, length), np.float32)
    backward = np.zeros((count, 2, 2, 4, 2, 4, length), np.float32)
    for i in range(4):
        forward[:, :, i, i] = np.transpose(stacked * norm, (1, 0, 2))
        for h in range(2):
            backward[:, h, :, i, h, i] = np.transpose(stacked * (2 * norm), (1, 0, 2))
    forward = forward.reshape(count * 8, 4 * length)
    backward = backward.reshape(count * 16, 8 * length)
    return forward.astype(jnp.bfloat16), backward.astype(jnp.bfloat16)


def low_rows(shape):
    return lax.broadcasted_iota(jnp.int32, shape, len(shape) - 2) < 4


def interleave(first, second):
    axis = first.ndim - 2
    low = low_rows(first.shape)
    top = jnp.where(low, first, pltpu.roll(second, 4, axis))
    bottom = jnp.where(low, pltpu.roll(first, 4, axis), second)
    return top, bottom


def exchange_kernel(
    scale,
    traces,
    table,
    weights,
    out,
    tr,
    tbl,
    S,
    T,
    R,
    A,
    B,
    W,
    O,
    T2,
    tr_sem,
    tbl_sem,
    in1,
    in2,
    ret1,
    ret2,
    send,
    xr_sem,
    n_sem,
    dp_sem,
    d_sem,
    core_sem,
    own_sem,
):
    x = lax.axis_index("freq")
    z = lax.axis_index("row")
    col = lax.axis_index("col")
    y = col // 2
    c = col % 2
    uy, uz = y % 2, z % 2
    Y, Z = y // 2, z // 2
    u = uy * 2 + uz

    def dev(xx, zz, yy, cc):
        return (xx, zz, yy * 2 + cc)

    def along(axis_pos, other_pos, core):
        return (
            jnp.where(core == 0, axis_pos, other_pos),
            jnp.where(core == 0, other_pos, axis_pos),
        )

    def remote(src, dst, s, r, to):
        return pltpu.make_async_remote_copy(
            src_ref=src, dst_ref=dst, send_sem=s, recv_sem=r, device_id=to, device_id_type=MESH
        )

    def wait_bytes(ref, sem):
        pltpu.make_async_copy(ref, ref, sem).wait()

    tbl_copy = pltpu.make_async_copy(table, tbl, tbl_sem)
    tbl_copy.start()
    for k in range(8):
        pltpu.make_async_copy(traces.at[:, pl.ds(k * 256, 256), :], tr.at[k], tr_sem.at[k]).start()

    barrier = pltpu.get_barrier_semaphore()
    partner = dev(x, z, y, 1 - c)
    left = dev((x + 3) % 4, z, y, c)
    right = dev((x + 1) % 4, z, y, c)
    yn = dev(x, z, y + 1 - 2 * uy, c)
    zn = dev(x, z + 1 - 2 * uz, y, c)
    dn = dev(x, z + 1 - 2 * uz, y + 1 - 2 * uy, c)

    def greet(d, carry):
        for core in range(2):
            pl.semaphore_signal(barrier, inc=1, device_id=dev(x, z, (y + d) % 8, core), device_id_type=MESH)
            pl.semaphore_signal(barrier, inc=1, device_id=dev(x, (z + d) % 8, y, core), device_id_type=MESH)
        return carry

    lax.fori_loop(1, 8, greet, 0)
    for other in (partner, left, right, dn):
        pl.semaphore_signal(barrier, inc=1, device_id=other, device_id_type=MESH)

    tbl_copy.wait()

    def transform(core, v):
        k = core * 4 + v
        pltpu.make_async_copy(tr.at[k], tr.at[k], tr_sem.at[k]).wait()
        block = jnp.concatenate([tr[k, s] for s in range(4)], axis=1)
        data = lax.dot_general(tbl[...], block, (((1,), (1,)), ((), ())), preferred_element_type=F32)
        data = data.reshape(16, 8, 256)
        data = jnp.concatenate([data[:, :, :128], data[:, :, 128:]], axis=1)
        data = data.astype(BF16).reshape(4, 4, 16, 128)
        for first in range(4):
            if core == 0:
                S[first, :, v] = data[first]
            else:
                S[4:8, first, v] = data[first]

    for v in range(4):
        transform(0, v)
    pl.semaphore_wait(barrier, 32)

    for d in range(1, 4):
        to = (Y + d) % 4
        remote(S.at[to], T.at[:, Y, c], send.at[0], in1, dev(x, z, 2 * to + uy, 0)).start()

    @pl.when(c == 0)
    def _():
        pltpu.make_async_copy(S.at[Y], T.at[:, Y, c], in1).start()

    @pl.when(c == 1)
    def _():
        remote(S.at[Y], T.at[:, Y, c], send.at[0], in1, partner).start()

    for v in range(4):
        transform(1, v)
    for d in range(1, 4):
        to = (Z + d) % 4
        remote(S.at[4 + to], T.at[:, Z, c], send.at[0], in1, dev(x, 2 * to + uz, y, 1)).start()

    @pl.when(c == 1)
    def _():
        pltpu.make_async_copy(S.at[4 + Z], T.at[:, Z, c], in1).start()

    @pl.when(c == 0)
    def _():
        remote(S.at[4 + Z], T.at[:, Z, c], send.at[0], in1, partner).start()

    wait_bytes(T, in1)

    b4 = jnp.where(c == 0, Z, Y)
    for d in range(1, 4):
        to = (b4 + d) % 4
        far = 2 * to + jnp.where(c == 0, uz, uy)
        yy = jnp.where(c == 0, y, far)
        zz = jnp.where(c == 0, far, z)
        remote(T.at[to], R.at[b4], send.at[1], in2, dev(x, zz, yy, c)).start()
    pltpu.make_async_copy(T.at[b4], R.at[b4], in2).start()
    wait_bytes(R, in2)

    def settle(n, carry):
        b, a = n // 4, n % 4
        row = pl.multiple_of(jnp.where(c == 0, a * 4 + b, n) * 16, 16)
        first = R[b, a, 0].astype(F32).reshape(4, 2, 8, 128)
        second = R[b, a, 1].astype(F32).reshape(4, 2, 8, 128)
        real, imag = interleave(first, second)
        for v in range(4):
            for h in range(2):
                tile = jnp.concatenate([real[v, h], imag[v, h]], axis=0).astype(BF16)
                A[c, u, pl.ds(row, 16), v * 256 + h * 128 : v * 256 + h * 128 + 128] = tile
        return carry

    lax.fori_loop(0, 16, settle, 0)

    def lanes(v):
        return pl.ds(pl.multiple_of(v * 256, 256), 256)

    def panel(m, v):
        return A.at[c, m, :, lanes(v)]

    def x_send(m):
        remote(panel(m, u), B.at[x, m], send.at[2], xr_sem.at[0, m], right).start()
        remote(panel(m, u), B.at[x, m], send.at[2], xr_sem.at[1, m], left).start()

    def n_send(which, v):
        remote(panel(u, v), panel(u, v), send.at[3], n_sem.at[which, v], (yn, zn)[which]).start()

    def core_send(ref):
        remote(ref, ref, send.at[4], core_sem, partner).start()

    my, mz, md = u ^ 2, u ^ 1, u ^ 3
    x_send(u)
    n_send(0, my)
    n_send(1, mz)
    remote(panel(u, md), panel(u, md), send.at[3], dp_sem, dn).start()
    core_send(A.at[c, u])
    n_send(0, u)
    n_send(1, u)
    n_send(0, mz)
    n_send(1, my)
    n_send(0, md)
    n_send(1, md)

    def n_arrive(which, v, forward):
        m = (my, mz)[which]
        wait_bytes(panel(m, v), n_sem.at[which, v])
        if forward:
            half = A.at[c, m, pl.ds(which * 128, 128), lanes(v)]
            remote(half, half, send.at[3], d_sem.at[which, v], (zn, yn)[which]).start()
        core_send(panel(m, v))

    n_arrive(0, u, True)
    x_send(my)
    n_arrive(1, u, True)
    x_send(mz)
    wait_bytes(panel(md, u), dp_sem)
    x_send(md)
    core_send(panel(md, u))
    pltpu.make_async_copy(A.at[c, :, :, lanes(u)], B.at[x], own_sem).start()

    xl, xr, xo = (x + 3) % 4, (x + 1) % 4, (x + 2) % 4

    def x_arrive(m, odd):
        wait_bytes(B.at[xl, m], xr_sem.at[0, m])
        if not odd:
            remote(B.at[xl, m], B.at[xl, m], send.at[2], xr_sem.at[2, m], right).start()
        wait_bytes(B.at[xr, m], xr_sem.at[1, m])
        if odd:
            remote(B.at[xr, m], B.at[xr, m], send.at[2], xr_sem.at[2, m], left).start()

    x_arrive(u, False)
    n_arrive(0, my, True)
    n_arrive(1, mz, True)
    x_arrive(my, True)
    n_arrive(0, md, True)
    n_arrive(1, md, True)
    x_arrive(mz, False)
    n_arrive(0, mz, False)
    n_arrive(1, my, False)
    x_arrive(md, True)

    def regroup(xp):
        def step(n, carry):
            uz_, Z_, Y_ = n // 16, (n // 4) % 4, n % 4
            row = pl.multiple_of((Y_ * 4 + Z_) * 16, 16)
            even = B[xp, uz_, pl.ds(row, 16), :].astype(F32)
            odd = B[xp, 2 + uz_, pl.ds(row, 16), :].astype(F32)
            at = pl.ds(pl.multiple_of((2 * Z_ + uz_) * 64 + Y_ * 16, 16), 16)
            W[xp, at, 0:256] = jnp.concatenate([even[:8], odd[:8]], axis=0).astype(BF16)
            W[xp, at, 256:512] = jnp.concatenate([even[8:], odd[8:]], axis=0).astype(BF16)
            return carry

        lax.fori_loop(0, 32, step, 0, unroll=4)

    wait_bytes(B.at[x], own_sem)
    regroup(x)
    regroup(xl)
    regroup(xr)
    for m in (u, my, mz, md):
        wait_bytes(B.at[xo, m], xr_sem.at[2, m])
    regroup(xo)
    for v in (u ^ 1, u ^ 2, u ^ 3):
        for which in range(2):
            half = A.at[c, md, pl.ds(which * 128, 128), lanes(v)]
            wait_bytes(half, d_sem.at[which, v])
            core_send(half)
    wait_bytes(A.at[1 - c], core_sem)

    j = Y * 4 + Z
    w_real, w_imag = weights[0, j], weights[1, j]

    def multiply(m, carry):
        my_, mz_ = m // 2, m % 2
        total = jnp.dot(A[0, m], W[0:2].reshape(1024, 512), preferred_element_type=F32)
        total += jnp.dot(A[1, m], W[2:4].reshape(1024, 512), preferred_element_type=F32)
        total = total.reshape(16, 2, 8, 512)
        real = total[:, 0, :, :256] - total[:, 1, :, 256:]
        imag = total[:, 0, :, 256:] + total[:, 1, :, :256]
        pred_real = (w_real * real - w_imag * imag) * scale
        pred_imag = (w_real * imag + w_imag * real) * scale
        for core, part in enumerate(interleave(pred_real, pred_imag)):
            part = jnp.concatenate([part[:, :, :128], part[:, :, 128:]], axis=1).astype(BF16)
            for n in range(16):
                yy, zz = 2 * (n // 4) + my_, 2 * (n % 4) + mz_
                if core == 0:
                    O[yy, zz] = part[n]
                else:
                    O[8 + zz, yy] = part[n]
        return carry

    lax.fori_loop(0, 4, multiply, 0)

    def back1(d, carry):
        yy, zz = (y + d) % 8, (z + d) % 8
        remote(O.at[yy], T2.at[:, y, c], send.at[5], ret1, dev(x, z, yy, 0)).start()
        remote(O.at[8 + zz], T2.at[:, z, c], send.at[5], ret1, dev(x, zz, y, 1)).start()
        return carry

    lax.fori_loop(1, 8, back1, 0)

    @pl.when(c == 0)
    def _():
        pltpu.make_async_copy(O.at[y], T2.at[:, y, c], ret1).start()
        remote(O.at[8 + z], T2.at[:, z, c], send.at[5], ret1, partner).start()

    @pl.when(c == 1)
    def _():
        pltpu.make_async_copy(O.at[8 + z], T2.at[:, z, c], ret1).start()
        remote(O.at[y], T2.at[:, y, c], send.at[5], ret1, partner).start()

    wait_bytes(T2, ret1)

    b8 = jnp.where(c == 0, z, y)

    def back2(d, carry):
        to = (b8 + d) % 8
        yy = jnp.where(c == 0, y, to)
        zz = jnp.where(c == 0, to, z)
        remote(T2.at[to], out.at[b8], send.at[6], ret2, dev(x, zz, yy, c)).start()
        return carry

    lax.fori_loop(1, 8, back2, 0)
    pltpu.make_async_copy(T2.at[b8], out.at[b8], ret2).start()
    wait_bytes(out, ret2)

    wait_bytes(S.at[pl.ds(0, 7)], send.at[0])
    wait_bytes(T.at[pl.ds(0, 3)], send.at[1])
    wait_bytes(B.at[pl.ds(0, 3)], send.at[2])
    wait_bytes(A.at[0, pl.ds(0, 3)], send.at[3])
    wait_bytes(A.at[0], send.at[4])
    wait_bytes(O.at[pl.ds(0, 15)], send.at[5])
    wait_bytes(T2.at[pl.ds(0, 7)], send.at[6])


def restore_kernel(spectra, table, out):
    n = pl.program_id(0)
    core, uy, uz = n // 4, (n // 2) % 2, n % 2
    c = lax.axis_index("col") % 2
    tiles = []
    for j in range(16):
        y, z = 2 * (j // 4) + uy, 2 * (j % 4) + uz
        b, a = jnp.where(c == 0, z, y), jnp.where(c == 0, y, z)
        tiles.append(spectra[b, a, core])
    left = jnp.concatenate(tiles, axis=0)
    traces = lax.dot_general(left, table[...], (((0,), (0,)), ((), ())), preferred_element_type=F32)
    traces = traces.astype(BF16)
    for h in range(2):
        for s in range(4):
            k = (h * 4 + s) * 128
            out[s, h * 128 : h * 128 + 128, :] = traces[:, k : k + 128]


def on_device(forward, backward, traces, source_inverse):
    hbm = pl.BlockSpec(memory_space=pl.ANY)
    dma = pltpu.SemaphoreType.DMA
    width = traces.shape[1]
    spectra = pl.pallas_call(
        functools.partial(exchange_kernel, 1.0 / math.sqrt(width)),
        out_shape=jax.ShapeDtypeStruct((8, 8, 2, 16, 128), BF16),
        in_specs=[hbm, hbm, pl.BlockSpec(memory_space=pltpu.SMEM)],
        out_specs=hbm,
        scratch_shapes=[
            pltpu.VMEM((8, 4, 256, 128), BF16),
            pltpu.VMEM((128, 512), BF16),
            pltpu.VMEM((8, 4, 4, 16, 128), BF16),
            pltpu.VMEM((4, 4, 2, 4, 16, 128), BF16),
            pltpu.VMEM((4, 4, 2, 4, 16, 128), BF16),
            pltpu.VMEM((2, 4, 256, 1024), BF16),
            pltpu.VMEM((4, 4, 256, 256), BF16),
            pltpu.VMEM((4, 512, 512), BF16),
            pltpu.VMEM((16, 8, 16, 128), BF16),
            pltpu.VMEM((8, 8, 2, 16, 128), BF16),
            dma((8,)),
            dma(()),
            dma(()),
            dma(()),
            dma(()),
            dma(()),
            dma((7,)),
            dma((3, 4)),
            dma((2, 4)),
            dma(()),
            dma((2, 4)),
            dma(()),
            dma(()),
        ],
        compiler_params=pltpu.CompilerParams(
            collective_id=0, has_side_effects=True, vmem_limit_bytes=VMEM_LIMIT
        ),
        name="exchange",
    )(traces, jnp.asarray(forward), source_inverse)
    return pl.pallas_call(
        restore_kernel,
        grid=(8,),
        out_shape=jax.ShapeDtypeStruct(traces.shape, BF16),
        in_specs=[
            pl.BlockSpec((8, 8, 2, 16, 128), lambda n: (0, 0, 0, 0, 0)),
            pl.BlockSpec((256, 1024), lambda n: (0, 0)),
        ],
        out_specs=pl.BlockSpec((4, 256, 128), lambda n: (0, n, 0)),
        compiler_params=pltpu.CompilerParams(vmem_limit_bytes=VMEM_LIMIT),
        name="restore",
    )(spectra, jnp.asarray(backward))


def solution(mesh):
    forward, backward = tables(16, 128)
    in_specs = (P(("freq", "row", "col"), None, None), P())
    out_specs = P(("freq", "row", "col"), None, None)
    return jax.shard_map(
        functools.partial(on_device, forward, backward),
        mesh=mesh,
        in_specs=in_specs,
        out_specs=out_specs,
        check_vma=False,
    )
```

time: 211 us -> 85.5 us (0.41)
  waiting for transfers between devices: 121 us -> 0 us
  Pallas kernels: 0 us -> 82.2 us
  blocking collectives: 51.2 us -> 0 us
  between operations: 13.5 us -> 0.02 us
  local copies, waits for them, and re-layouts: 13.4 us -> 3.18 us
  matrix products: 9.14 us -> 0 us
    all_gather x2 -> x0, waiting for transfers between devices: 120 us -> none  [the longest x1 62.7 us: on_device(): lax.all_gather(local_block, 'col', axis=3, tiled=True)]
    pallas_call x0 -> x2, Pallas kernels: none -> 82.2 us  [the longest x1 77.7 us: on_device(): pl.pallas_call(functools.partial(exchange_kernel, 1.0 / math.sqrt(width))...]
    all_to_all x2 -> x0, blocking collectives: 51.2 us -> none  [the longest x1 28.7 us: on_device(): lax.all_to_all(spectra, ('freq', 'col'), split_axis=0, concat_axis=0, til...]
    dot_general x3 -> x0, matrix products: 9.14 us -> none  [the longest x1 7.29 us: complex_block(): jnp.einsum('pjik,qjkl->pqjil', left, right, preferred_element_type=jnp.fl...]
    reshape x3 -> x0, local copies, waits for them, and re-layouts: 7.34 us -> none  [the longest x1 6.53 us: on_device(): column_panel.reshape(2, band, rows, cols, groups, shots, block)]
  transfers between devices with their start and end apart: 2 -> 0, of which waited for: 2 -> 0; matrix products, arithmetic and copies ran while one was open for 3% -> 0% of each run, Pallas kernels for 0% -> 0%
where the time goes in v1:
time: 85.5 us; the launch traced here: 85.4 us
  Pallas kernels  82.2 us (96%)
  local copies, waits for them, and re-layouts  3.18 us (4%)
    pallas_call x1, Pallas kernels, on_device(): pl.pallas_call(functools.partial(exchange_kernel, 1.0 / math.sqrt(width))...  77.7 us
    pallas_call x1, Pallas kernels, on_device(): pl.pallas_call(restore_kernel, grid=(8,), out_shape=jax.ShapeDtypeStruct(...  4.45 us
    unnamed x8, local copies, waits for them, and re-layouts  3.18 us

profile of v1, /device:TPU:1, one launch (start us, length us, event | category | flops | bytes accessed | tf_op | source)
XLA Modules:
  0.0 85.4 jit_solution(11096061048650534573)
XLA Ops:
  0.0 0.0 copy-start
  0.0 1.6 %copy-done = bf16[4,2048,128]{2,1,0:T(8,128)(2,1)S(1)} copy-done((bf16[4,2048,128]{2,1,0:T(8,128)(2,1)S(1)}, bf16[4,2048,128]{2,1,0:T(8,128)(2,1)}, u32[]{:S(2)}) %copy-start) | copy-done | bytes 2097176
  1.6 0.0 copy-start.2
  1.6 0.9 %copy-done.2 = bf16[128,512]{1,0:T(8,128)(2,1)S(1)} copy-done((bf16[128,512]{1,0:T(8,128)(2,1)S(1)}, bf16[128,512]{1,0:T(8,128)(2,1)}, u32[]{:S(2)}) %copy-start.2) | copy-done | bytes 131096
  2.5 0.0 copy-start.3
  2.5 0.7 copy-done.3
  3.2 0.0 copy-start.1
  3.2 77.7 %exchange.1.spectra = bf16[8,8,2,16,128]{4,3,2,1,0:T(8,128)(2,1)S(1)} custom-call(bf16[4,2048,128]{2,1,0:T(8,128)(2,1)S(1)} %copy-done, bf16[128,512]{1,0:T(8,128)(2,1)S(1)} %copy-done.2, f32[2,16]{1,0:T(2,128)S(1)} %copy-done.3), custom_call_target="tpu_custom_call" | custom-call | tf_op jit(solution)/shard_map/exchange/pallas_call | solution.py:381
  80.9 0.0 copy-done.1
  80.9 4.4 %restore.1 = bf16[4,2048,128]{2,1,0:T(8,128)(2,1)} custom-call(bf16[8,8,2,16,128]{4,3,2,1,0:T(8,128)(2,1)S(1)} %exchange.1.spectra, bf16[256,1024]{1,0:T(8,128)(2,1)S(1)} %copy-done.1), custom_call_target="tpu_custom_call" | custom-call | tf_op jit(solution)/shard_map/restore/pallas_call | solution.py:416
Async XLA Ops:
  0.0 1.6 %copy-start = (bf16[4,2048,128]{2,1,0:T(8,128)(2,1)S(1)}, bf16[4,2048,128]{2,1,0:T(8,128)(2,1)}, u32[]{:S(2)}) copy-start(bf16[4,2048,128]{2,1,0:T(8,128)(2,1)} %traces.1) | copy-start | bytes 6291460
  1.6 0.9 %copy-start.2 = (bf16[128,512]{1,0:T(8,128)(2,1)S(1)}, bf16[128,512]{1,0:T(8,128)(2,1)}, u32[]{:S(2)}) copy-start(bf16[128,512]{1,0:T(8,128)(2,1)} %constant.4.clone.table) | copy-start | bytes 393220
  2.5 0.7 copy-start.3
  3.2 77.7 %copy-start.1 = (bf16[256,1024]{1,0:T(8,128)(2,1)S(1)}, bf16[256,1024]{1,0:T(8,128)(2,1)}, u32[]{:S(2)}) copy-start(bf16[256,1024]{1,0:T(8,128)(2,1)} %constant.5.clone.table) | copy-start | bytes 1572868

commit v2 on v0

v2 whole, which is shorter than its diff:
```python
import functools
import math

import jax
import jax.numpy as jnp
import numpy as np
from jax import lax
from jax.experimental import pallas as pl
from jax.experimental.pallas import tpu as pltpu
from jax.sharding import PartitionSpec as P

MESH = pl.DeviceIdType.MESH
BF16 = jnp.bfloat16
F32 = jnp.float32
VMEM_LIMIT = 62 * 1024 * 1024 + 512 * 1024


def tables(count, length):
    bins = np.arange(count, dtype=np.int32) + 1
    times = np.arange(length, dtype=np.int32)
    index = bins[:, None] * times[None, :] % length
    angle = index.astype(np.float32) * np.float32(2.0 * math.pi / length)
    norm = np.float32(1.0 / math.sqrt(length))
    stacked = np.stack([np.cos(angle), -np.sin(angle)])
    forward = np.zeros((count, 2, 4, 4, length), np.float32)
    backward = np.zeros((count, 2, 2, 4, 2, 4, length), np.float32)
    for i in range(4):
        forward[:, :, i, i] = np.transpose(stacked * norm, (1, 0, 2))
        for h in range(2):
            backward[:, h, :, i, h, i] = np.transpose(stacked * (2 * norm), (1, 0, 2))
    forward = forward.reshape(count * 8, 4 * length)
    backward = backward.reshape(count * 16, 8 * length)
    return forward.astype(jnp.bfloat16), backward.astype(jnp.bfloat16)


def low_rows(shape):
    return lax.broadcasted_iota(jnp.int32, shape, len(shape) - 2) < 4


def interleave(first, second):
    axis = first.ndim - 2
    low = low_rows(first.shape)
    top = jnp.where(low, first, pltpu.roll(second, 4, axis))
    bottom = jnp.where(low, pltpu.roll(first, 4, axis), second)
    return top, bottom


def exchange_kernel(
    scale,
    traces,
    table,
    source,
    out,
    tr,
    tbl,
    weights,
    S,
    T,
    R,
    A,
    B,
    W,
    O,
    T2,
    tr_sem,
    tbl_sem,
    src_sem,
    in1,
    in2,
    ret1,
    ret2,
    send,
    x_sem,
    n_sem,
    dp_sem,
    d_sem,
    core_sem,
    own_sem,
):
    x = lax.axis_index("freq")
    z = lax.axis_index("row")
    col = lax.axis_index("col")
    y = col // 2
    c = col % 2
    uy, uz = y % 2, z % 2
    Y, Z = y // 2, z // 2
    u = uy * 2 + uz

    def dev(xx, zz, yy, cc):
        return (xx, zz, yy * 2 + cc)

    def remote(src, dst, s, r, to):
        return pltpu.make_async_remote_copy(
            src_ref=src, dst_ref=dst, send_sem=s, recv_sem=r, device_id=to, device_id_type=MESH
        )

    def local(src, dst, s):
        return pltpu.make_async_copy(src, dst, s)

    def wait_bytes(ref, sem):
        pltpu.make_async_copy(ref, ref, sem).wait()

    local(table, tbl, tbl_sem).start()
    for h in range(2):
        for k in range(4):
            local(traces.at[:, pl.ds(2 * k, 2), h], tr.at[h, k], tr_sem.at[h, k]).start()
    local(source, weights, src_sem).start()

    barrier = pltpu.get_barrier_semaphore()
    partner = dev(x, z, y, 1 - c)
    left = dev((x + 3) % 4, z, y, c)
    right = dev((x + 1) % 4, z, y, c)
    yn = dev(x, z, y + 1 - 2 * uy, c)
    zn = dev(x, z + 1 - 2 * uz, y, c)
    dn = dev(x, z + 1 - 2 * uz, y + 1 - 2 * uy, c)

    def greet(d, carry):
        for core in range(2):
            pl.semaphore_signal(barrier, inc=1, device_id=dev(x, z, (y + d) % 8, core), device_id_type=MESH)
            pl.semaphore_signal(barrier, inc=1, device_id=dev(x, (z + d) % 8, y, core), device_id_type=MESH)
        return carry

    lax.fori_loop(1, 8, greet, 0)
    for other in (partner, left, right, dn):
        pl.semaphore_signal(barrier, inc=1, device_id=other, device_id_type=MESH)

    def transform(h, core):
        for w in range(2):
            k = core * 2 + w
            wait_bytes(tr.at[h, k], tr_sem.at[h, k])
            block = jnp.concatenate([tr[h, k, s].reshape(256, 128) for s in range(4)], axis=1)
            data = lax.dot_general(tbl[...], block, (((1,), (1,)), ((), ())), preferred_element_type=F32)
            data = data.reshape(16, 8, 256)
            data = jnp.concatenate([data[:, :, :128], data[:, :, 128:]], axis=1)
            data = data.astype(BF16).reshape(4, 4, 16, 128)
            for first in range(4):
                if core == 0:
                    S[h, first, :, w] = data[first]
                else:
                    S[h, 4:8, first, w] = data[first]

    def scatter(h):
        for d in range(1, 4):
            to = (Y + d) % 4
            remote(S.at[h, to], T.at[h, :, Y, c], send.at[h], in1.at[h], dev(x, z, 2 * to + uy, 0)).start()
            to = (Z + d) % 4
            remote(S.at[h, 4 + to], T.at[h, :, Z, c], send.at[h], in1.at[h], dev(x, 2 * to + uz, y, 1)).start()

        @pl.when(c == 0)
        def _():
            local(S.at[h, Y], T.at[h, :, Y, c], in1.at[h]).start()
            remote(S.at[h, 4 + Z], T.at[h, :, Z, c], send.at[h], in1.at[h], partner).start()

        @pl.when(c == 1)
        def _():
            local(S.at[h, 4 + Z], T.at[h, :, Z, c], in1.at[h]).start()
            remote(S.at[h, Y], T.at[h, :, Y, c], send.at[h], in1.at[h], partner).start()

    def scatter2(h):
        wait_bytes(T.at[h], in1.at[h])
        b4 = jnp.where(c == 0, Z, Y)
        for d in (1, 3, 2):
            to = (b4 + d) % 4
            far = 2 * to + jnp.where(c == 0, uz, uy)
            yy = jnp.where(c == 0, y, far)
            zz = jnp.where(c == 0, far, z)
            remote(T.at[h, to], R.at[h, b4], send.at[2 + h], in2.at[h], dev(x, zz, yy, c)).start()
        local(T.at[h, b4], R.at[h, b4], in2.at[h]).start()

    def settle(h):
        wait_bytes(R.at[h], in2.at[h])

        def step(n, carry):
            b, a = n // 4, n % 4
            row = pl.multiple_of(jnp.where(c == 0, a * 4 + b, n) * 16, 16)
            first = R[h, b, a, 0].astype(F32).reshape(2, 2, 8, 128)
            second = R[h, b, a, 1].astype(F32).reshape(2, 2, 8, 128)
            real, imag = interleave(first, second)
            for v in range(4):
                tile = jnp.concatenate([real[v // 2, v % 2], imag[v // 2, v % 2]], axis=0).astype(BF16)
                A[c, u, pl.ds(row, 16), v * 256 + h * 128 : v * 256 + h * 128 + 128] = tile
            return carry

        lax.fori_loop(0, 16, step, 0, unroll=2)

    my, mz, md = u ^ 2, u ^ 1, u ^ 3
    xl, xr, xo = (x + 3) % 4, (x + 1) % 4, (x + 2) % 4

    def lanes(v, h):
        return pl.ds(pl.multiple_of(v * 256 + h * 128, 128), 128)

    def panel(m, v, h):
        return A.at[c, m, :, lanes(v, h)]

    def x_send(m, h):
        remote(panel(m, u, h), B.at[x, h, m], send.at[4], x_sem.at[0, h, m], right).start()
        remote(panel(m, u, h), B.at[x, h, m], send.at[4], x_sem.at[1, h, m], left).start()

    def n_send(which, v, h):
        ref = panel(u, v, h)
        remote(ref, ref, send.at[5], n_sem.at[which, v, h], (yn, zn)[which]).start()

    def core_send(m, ref):
        remote(ref, ref, send.at[6], core_sem.at[m], partner).start()

    def first_sends(h):
        x_send(u, h)
        n_send(0, my, h)
        n_send(1, mz, h)
        remote(panel(u, md, h), panel(u, md, h), send.at[5], dp_sem.at[h], dn).start()

    def rest_sends(h):
        n_send(0, u, h)
        n_send(1, u, h)
        n_send(0, mz, h)
        n_send(1, my, h)
        n_send(0, md, h)
        n_send(1, md, h)

    def n_arrive(which, v, h, forward):
        m = (my, mz)[which]
        wait_bytes(panel(m, v, h), n_sem.at[which, v, h])
        if forward:
            half = A.at[c, m, pl.ds(which * 128, 128), lanes(v, h)]
            remote(half, half, send.at[5], d_sem.at[which, v, h], (zn, yn)[which]).start()
        core_send(m, panel(m, v, h))

    def first_arrive(h):
        n_arrive(0, u, h, True)
        x_send(my, h)
        n_arrive(1, u, h, True)
        x_send(mz, h)
        wait_bytes(panel(md, u, h), dp_sem.at[h])
        x_send(md, h)
        core_send(md, panel(md, u, h))
        local(A.at[c, :, :, lanes(u, h)], B.at[x, h], own_sem.at[h]).start()

    def x_arrive(m, h, odd):
        wait_bytes(B.at[xl, h, m], x_sem.at[0, h, m])
        if not odd:
            remote(B.at[xl, h, m], B.at[xl, h, m], send.at[4], x_sem.at[2, h, m], right).start()
        wait_bytes(B.at[xr, h, m], x_sem.at[1, h, m])
        if odd:
            remote(B.at[xr, h, m], B.at[xr, h, m], send.at[4], x_sem.at[2, h, m], left).start()

    def d_arrive(h):
        for r in (1, 2, 3):
            v = u ^ r
            for which in range(2):
                half = A.at[c, md, pl.ds(which * 128, 128), lanes(v, h)]
                wait_bytes(half, d_sem.at[which, v, h])
                core_send(md, half)

    def regroup(xp, h):
        def step(n, carry):
            uz_, Z_, Y_ = n // 16, (n // 4) % 4, n % 4
            row = pl.multiple_of((Y_ * 4 + Z_) * 16, 16)
            even = B[xp, h, uz_, pl.ds(row, 16), :].astype(F32)
            odd = B[xp, h, 2 + uz_, pl.ds(row, 16), :].astype(F32)
            at = pl.ds(pl.multiple_of((2 * Z_ + uz_) * 64 + Y_ * 16, 16), 16)
            W[xp, at, h * 128 : h * 128 + 128] = jnp.concatenate([even[:8], odd[:8]], axis=0).astype(BF16)
            W[xp, at, 256 + h * 128 : 384 + h * 128] = jnp.concatenate([even[8:], odd[8:]], axis=0).astype(BF16)
            return carry

        lax.fori_loop(0, 32, step, 0, unroll=8)

    j = Y * 4 + Z

    def multiply(at, flip):
        m = u ^ flip
        wait_bytes(A.at[1 - c, m], core_sem.at[m])
        w_real, w_imag = weights[0, j], weights[1, j]
        total = jnp.dot(A[0, m], W[0:2].reshape(1024, 512), preferred_element_type=F32)
        total += jnp.dot(A[1, m], W[2:4].reshape(1024, 512), preferred_element_type=F32)
        total = total.reshape(16, 2, 8, 512)
        real = total[:, 0, :, :256] - total[:, 1, :, 256:]
        imag = total[:, 0, :, 256:] + total[:, 1, :, :256]
        pred_real = (w_real * real - w_imag * imag) * scale
        pred_imag = (w_real * imag + w_imag * real) * scale
        for core, part in enumerate(interleave(pred_real, pred_imag)):
            part = jnp.concatenate([part[:, :, :128], part[:, :, 128:]], axis=1).astype(BF16)
            part = part.reshape(4, 4, 16, 128)
            for first in range(4):
                if core == 0:
                    O[at * 8 + first] = part[first]
                else:
                    O[at * 8 + 4 : at * 8 + 8, first] = part[first]

        uy_, uz_ = uy ^ (flip // 2), uz ^ (flip % 2)
        to_y = T2.at[pl.ds(uz_ * 4, 4), y, c]
        to_z = T2.at[pl.ds(uy_ * 4, 4), z, c]
        y_done, z_done = ret1.at[uz_, uy], ret1.at[uy_, uz]
        for d in (1, 3, 2, 0):
            to = (Y + d) % 4
            ref = O.at[at * 8 + to]
            if d == 0 and flip // 2 == 0:

                @pl.when(c == 0)
                def _():
                    local(ref, to_y, y_done).start()

                @pl.when(c == 1)
                def _():
                    remote(ref, to_y, send.at[7], y_done, partner).start()
            else:
                remote(ref, to_y, send.at[7], y_done, dev(x, z, 2 * to + uy_, 0)).start()
            to = (Z + d) % 4
            ref2 = O.at[at * 8 + 4 + to]
            if d == 0 and flip % 2 == 0:

                @pl.when(c == 1)
                def _():
                    local(ref2, to_z, z_done).start()

                @pl.when(c == 0)
                def _():
                    remote(ref2, to_z, send.at[7], z_done, partner).start()
            else:
                remote(ref2, to_z, send.at[7], z_done, dev(x, 2 * to + uz_, y, 1)).start()

    def back2(flip):
        b8 = jnp.where(c == 0, z, y)
        half, parity = b8 // 2, (b8 % 2) ^ flip
        for side in range(2):
            wait_bytes(O.at[pl.ds(0, 8)], ret1.at[parity, side])
        for d in (1, 3, 2, 0):
            to = (half + d) % 4
            ref = T2.at[parity * 4 + to]
            if d == 0 and flip == 0:
                local(ref, out.at[b8], ret2).start()
            else:
                far = 2 * to + parity
                yy = jnp.where(c == 0, y, far)
                zz = jnp.where(c == 0, far, z)
                remote(ref, out.at[b8], send.at[8], ret2, dev(x, zz, yy, c)).start()

    wait_bytes(tbl, tbl_sem)
    transform(0, 0)
    transform(0, 1)
    pl.semaphore_wait(barrier, 32)
    scatter(0)
    transform(1, 0)
    transform(1, 1)
    scatter(1)
    wait_bytes(weights, src_sem)
    scatter2(0)
    scatter2(1)
    settle(0)
    first_sends(0)
    rest_sends(0)
    first_arrive(0)
    settle(1)
    first_sends(1)
    core_send(u, A.at[c, u])
    rest_sends(1)
    x_arrive(u, 0, False)
    n_arrive(0, my, 0, True)
    n_arrive(1, mz, 0, True)
    x_arrive(my, 0, True)
    first_arrive(1)
    wait_bytes(B.at[x, 0], own_sem.at[0])
    regroup(x, 0)
    n_arrive(0, md, 0, True)
    n_arrive(1, md, 0, True)
    x_arrive(mz, 0, False)
    n_arrive(0, mz, 0, False)
    n_arrive(1, my, 0, False)
    x_arrive(md, 0, True)
    regroup(xl, 0)
    regroup(xr, 0)
    x_arrive(u, 1, False)
    n_arrive(0, my, 1, True)
    n_arrive(1, mz, 1, True)
    x_arrive(my, 1, True)
    wait_bytes(B.at[x, 1], own_sem.at[1])
    regroup(x, 1)
    n_arrive(0, md, 1, True)
    n_arrive(1, md, 1, True)
    x_arrive(mz, 1, False)
    n_arrive(0, mz, 1, False)
    n_arrive(1, my, 1, False)
    x_arrive(md, 1, True)
    regroup(xl, 1)
    regroup(xr, 1)
    d_arrive(0)
    for m in (u, my, mz, md):
        wait_bytes(B.at[xo, 0, m], x_sem.at[2, 0, m])
    regroup(xo, 0)
    for m in (u, my, mz, md):
        wait_bytes(B.at[xo, 1, m], x_sem.at[2, 1, m])
    regroup(xo, 1)
    multiply(0, 0)
    multiply(1, 2)
    d_arrive(1)
    multiply(2, 1)
    multiply(3, 3)
    back2(0)
    back2(1)
    wait_bytes(out, ret2)

    for h in range(2):
        wait_bytes(S.at[h, pl.ds(0, 7)], send.at[h])
        wait_bytes(T.at[h, pl.ds(0, 3)], send.at[2 + h])
    wait_bytes(B.at[pl.ds(0, 3)], send.at[4])
    wait_bytes(A.at[0, pl.ds(0, 3)], send.at[5])
    wait_bytes(A.at[0], send.at[6])
    wait_bytes(O.at[pl.ds(0, 30)], send.at[7])
    wait_bytes(T2.at[pl.ds(0, 7)], send.at[8])


def restore_kernel(spectra, table, out, held, sem):
    c = lax.axis_index("col") % 2
    copies = []
    for n in range(8):
        core, uy, uz = n // 4, (n // 2) % 2, n % 2
        tiles = []
        for j in range(16):
            y, z = 2 * (j // 4) + uy, 2 * (j % 4) + uz
            b, a = jnp.where(c == 0, z, y), jnp.where(c == 0, y, z)
            tiles.append(spectra[b, a, core])
        left = jnp.concatenate(tiles, axis=0)
        traces = lax.dot_general(left, table[...], (((0,), (0,)), ((), ())), preferred_element_type=F32)
        traces = traces.astype(BF16)
        for h in range(2):
            for s in range(4):
                k = (h * 4 + s) * 128
                held[s, n * 256 + h * 128 : n * 256 + h * 128 + 128, :] = traces[:, k : k + 128]
        rows = pl.ds(n * 256, 256)
        copy = pltpu.make_async_copy(held.at[:, rows, :], out.at[:, rows, :], sem.at[n])
        copy.start()
        copies.append(copy)
    for copy in copies:
        copy.wait()


def on_device(forward, backward, traces, source_inverse):
    hbm = pl.BlockSpec(memory_space=pltpu.HBM)
    vmem = pl.BlockSpec(memory_space=pltpu.VMEM)
    dma = pltpu.SemaphoreType.DMA
    width = traces.shape[1]
    spectra = pl.pallas_call(
        functools.partial(exchange_kernel, 1.0 / math.sqrt(width)),
        out_shape=jax.ShapeDtypeStruct((8, 8, 2, 16, 128), BF16),
        in_specs=[hbm, hbm, hbm],
        out_specs=vmem,
        scratch_shapes=[
            pltpu.VMEM((2, 4, 4, 2, 128, 128), BF16),
            pltpu.VMEM((128, 512), BF16),
            pltpu.SMEM((2, 16), F32),
            pltpu.VMEM((2, 8, 4, 2, 16, 128), BF16),
            pltpu.VMEM((2, 4, 4, 2, 2, 16, 128), BF16),
            pltpu.VMEM((2, 4, 4, 2, 2, 16, 128), BF16),
            pltpu.VMEM((2, 4, 256, 1024), BF16),
            pltpu.VMEM((4, 2, 4, 256, 128), BF16),
            pltpu.VMEM((4, 512, 512), BF16),
            pltpu.VMEM((32, 4, 16, 128), BF16),
            pltpu.VMEM((8, 8, 2, 16, 128), BF16),
            dma((2, 4)),
            dma(()),
            dma(()),
            dma((2,)),
            dma((2,)),
            dma((2, 2)),
            dma(()),
            dma((9,)),
            dma((3, 2, 4)),
            dma((2, 4, 2)),
            dma((2,)),
            dma((2, 4, 2)),
            dma((4,)),
            dma((2,)),
        ],
        compiler_params=pltpu.CompilerParams(
            collective_id=0, has_side_effects=True, vmem_limit_bytes=VMEM_LIMIT
        ),
        name="exchange",
    )(traces.reshape(4, 8, 2, 128, 128), jnp.asarray(forward), source_inverse)
    return pl.pallas_call(
        restore_kernel,
        out_shape=jax.ShapeDtypeStruct(traces.shape, BF16),
        in_specs=[vmem, vmem],
        out_specs=hbm,
        scratch_shapes=[pltpu.VMEM((4, width, 128), BF16), dma((8,))],
        compiler_params=pltpu.CompilerParams(vmem_limit_bytes=VMEM_LIMIT),
        name="restore",
    )(spectra, jnp.asarray(backward))


def solution(mesh):
    forward, backward = tables(16, 128)
    in_specs = (P(("freq", "row", "col"), None, None), P())
    out_specs = P(("freq", "row", "col"), None, None)
    return jax.shard_map(
        functools.partial(on_device, forward, backward),
        mesh=mesh,
        in_specs=in_specs,
        out_specs=out_specs,
        check_vma=False,
    )
```

time: 211 us -> 72.6 us (0.34)
  waiting for transfers between devices: 121 us -> 0 us
  Pallas kernels: 0 us -> 72.5 us
  blocking collectives: 51.2 us -> 0 us
  between operations: 13.5 us -> 0.01 us
  local copies, waits for them, and re-layouts: 13.4 us -> 0 us
  matrix products: 9.14 us -> 0 us
    all_gather x2 -> x0, waiting for transfers between devices: 120 us -> none  [the longest x1 62.7 us: on_device(): lax.all_gather(local_block, 'col', axis=3, tiled=True)]
    pallas_call x0 -> x2, Pallas kernels: none -> 72.5 us  [the longest x1 69.6 us: on_device(): pl.pallas_call(functools.partial(exchange_kernel, 1.0 / math.sqrt(width))...]
    all_to_all x2 -> x0, blocking collectives: 51.2 us -> none  [the longest x1 28.7 us: on_device(): lax.all_to_all(spectra, ('freq', 'col'), split_axis=0, concat_axis=0, til...]
    dot_general x3 -> x0, matrix products: 9.14 us -> none  [the longest x1 7.29 us: complex_block(): jnp.einsum('pjik,qjkl->pqjil', left, right, preferred_element_type=jnp.fl...]
    reshape x3 -> x0, local copies, waits for them, and re-layouts: 7.34 us -> none  [the longest x1 6.53 us: on_device(): column_panel.reshape(2, band, rows, cols, groups, shots, block)]
  transfers between devices with their start and end apart: 2 -> 0, of which waited for: 2 -> 0; matrix products, arithmetic and copies ran while one was open for 3% -> 0% of each run, Pallas kernels for 0% -> 0%
where the time goes in v2:
time: 72.6 us; the launch traced here: 72.5 us
  Pallas kernels  72.5 us (100%)
    pallas_call x1, Pallas kernels, on_device(): pl.pallas_call(functools.partial(exchange_kernel, 1.0 / math.sqrt(width))...  69.6 us
    pallas_call x1, Pallas kernels, on_device(): pl.pallas_call(restore_kernel, out_shape=jax.ShapeDtypeStruct(traces.shap...  2.88 us

profile of v2, /device:TPU:1, one launch (start us, length us, event | category | flops | bytes accessed | tf_op | source)
XLA Modules:
  0.0 72.5 jit_solution(6082868971699839426)
XLA Ops:
  0.0 69.6 %exchange.1.spectra = bf16[8,8,2,16,128]{4,3,2,1,0:T(8,128)(2,1)} custom-call(bf16[4,8,2,128,128]{4,3,2,1,0:T(8,128)(2,1)} %bitcast.1, bf16[128,512]{1,0:T(8,128)(2,1)} %constant.4.clone.table, f32[2,16]{1,0:T(2,128)} %source.1), custom_call_target="tpu_custom_call" | custom-call | tf_op jit(solution)/shard_map/exchange/pallas_call | solution.py:441
  69.6 2.9 %restore.1 = bf16[4,2048,128]{2,1,0:T(8,128)(2,1)} custom-call(bf16[8,8,2,16,128]{4,3,2,1,0:T(8,128)(2,1)} %exchange.1.spectra, bf16[256,1024]{1,0:T(8,128)(2,1)} %constant.5.clone.table), custom_call_target="tpu_custom_call" | custom-call | tf_op jit(solution)/shard_map/restore/pallas_call | solution.py:478

commit v3 on v2

--- a/solution.py
+++ b/solution.py
@@ -23,14 +23,10 @@
     norm = np.float32(1.0 / math.sqrt(length))
     stacked = np.stack([np.cos(angle), -np.sin(angle)])
     forward = np.zeros((count, 2, 4, 4, length), np.float32)
-    backward = np.zeros((count, 2, 2, 4, 2, 4, length), np.float32)
     for i in range(4):
         forward[:, :, i, i] = np.transpose(stacked * norm, (1, 0, 2))
-        for h in range(2):
-            backward[:, h, :, i, h, i] = np.transpose(stacked * (2 * norm), (1, 0, 2))
     forward = forward.reshape(count * 8, 4 * length)
-    backward = backward.reshape(count * 16, 8 * length)
-    return forward.astype(jnp.bfloat16), backward.astype(jnp.bfloat16)
+    return forward.astype(jnp.bfloat16), (2 * forward).astype(jnp.bfloat16)
 
 
 def low_rows(shape):
@@ -71,6 +67,7 @@
     ret2,
     send,
     x_sem,
+    p_sem,
     n_sem,
     dp_sem,
     d_sem,
@@ -113,15 +110,12 @@
     yn = dev(x, z, y + 1 - 2 * uy, c)
     zn = dev(x, z + 1 - 2 * uz, y, c)
     dn = dev(x, z + 1 - 2 * uz, y + 1 - 2 * uy, c)
-
-    def greet(d, carry):
-        for core in range(2):
-            pl.semaphore_signal(barrier, inc=1, device_id=dev(x, z, (y + d) % 8, core), device_id_type=MESH)
-            pl.semaphore_signal(barrier, inc=1, device_id=dev(x, (z + d) % 8, y, core), device_id_type=MESH)
-        return carry
-
-    lax.fori_loop(1, 8, greet, 0)
-    for other in (partner, left, right, dn):
+    others = [partner, left, right, yn, zn, dn]
+    for d in (2, 4, 6):
+        a_y, a_z = jnp.where(c == 0, (y + d) % 8, y), jnp.where(c == 0, z, (z + d) % 8)
+        b_y, b_z = jnp.where(c == 0, y, (y + d) % 8), jnp.where(c == 0, (z + d) % 8, z)
+        others += [dev(x, a_z, a_y, 0), dev(x, a_z, a_y, 1), dev(x, b_z, b_y, c)]
+    for other in others:
         pl.semaphore_signal(barrier, inc=1, device_id=other, device_id_type=MESH)
 
     def transform(h, core):
@@ -139,27 +133,36 @@
                 else:
                     S[h, 4:8, first, w] = data[first]
 
-    def scatter(h):
-        for d in range(1, 4):
+    def scatter_y(h):
+        for d in (2, 1, 3):
             to = (Y + d) % 4
             remote(S.at[h, to], T.at[h, :, Y, c], send.at[h], in1.at[h], dev(x, z, 2 * to + uy, 0)).start()
-            to = (Z + d) % 4
-            remote(S.at[h, 4 + to], T.at[h, :, Z, c], send.at[h], in1.at[h], dev(x, 2 * to + uz, y, 1)).start()
 
         @pl.when(c == 0)
         def _():
             local(S.at[h, Y], T.at[h, :, Y, c], in1.at[h]).start()
+
+        @pl.when(c == 1)
+        def _():
+            remote(S.at[h, Y], T.at[h, :, Y, c], send.at[h], in1.at[h], partner).start()
+
+    def scatter_z(h):
+        for d in (2, 1, 3):
+            to = (Z + d) % 4
+            remote(S.at[h, 4 + to], T.at[h, :, Z, c], send.at[h], in1.at[h], dev(x, 2 * to + uz, y, 1)).start()
+
+        @pl.when(c == 0)
+        def _():
             remote(S.at[h, 4 + Z], T.at[h, :, Z, c], send.at[h], in1.at[h], partner).start()
 
         @pl.when(c == 1)
         def _():
             local(S.at[h, 4 + Z], T.at[h, :, Z, c], in1.at[h]).start()
-            remote(S.at[h, Y], T.at[h, :, Y, c], send.at[h], in1.at[h], partner).start()
 
     def scatter2(h):
         wait_bytes(T.at[h], in1.at[h])
         b4 = jnp.where(c == 0, Z, Y)
-        for d in (1, 3, 2):
+        for d in (2, 1, 3):
             to = (b4 + d) % 4
             far = 2 * to + jnp.where(c == 0, uz, uy)
             yy = jnp.where(c == 0, y, far)
@@ -189,51 +192,48 @@
     def lanes(v, h):
         return pl.ds(pl.multiple_of(v * 256 + h * 128, 128), 128)
 
-    def panel(m, v, h):
-        return A.at[c, m, :, lanes(v, h)]
+    def panel(m, v, rows=pl.ds(0, 256)):
+        return A.at[c, m, rows, pl.ds(pl.multiple_of(v * 256, 256), 256)]
 
     def x_send(m, h):
-        remote(panel(m, u, h), B.at[x, h, m], send.at[4], x_sem.at[0, h, m], right).start()
-        remote(panel(m, u, h), B.at[x, h, m], send.at[4], x_sem.at[1, h, m], left).start()
-
-    def n_send(which, v, h):
-        ref = panel(u, v, h)
-        remote(ref, ref, send.at[5], n_sem.at[which, v, h], (yn, zn)[which]).start()
+        ref = A.at[c, m, :, lanes(u, h)]
+        remote(ref, B.at[x, h, m], send.at[4], x_sem.at[0, h, m], right).start()
+        remote(ref, B.at[x, h, m], send.at[4], x_sem.at[1, h, m], left).start()
 
     def core_send(m, ref):
         remote(ref, ref, send.at[6], core_sem.at[m], partner).start()
 
     def first_sends(h):
         x_send(u, h)
-        n_send(0, my, h)
-        n_send(1, mz, h)
-        remote(panel(u, md, h), panel(u, md, h), send.at[5], dp_sem.at[h], dn).start()
-
-    def rest_sends(h):
-        n_send(0, u, h)
-        n_send(1, u, h)
-        n_send(0, mz, h)
-        n_send(1, my, h)
-        n_send(0, md, h)
-        n_send(1, md, h)
-
-    def n_arrive(which, v, h, forward):
+        for ref, sem, to in (
+            (A.at[c, u, :, lanes(my, h)], p_sem.at[0, h], yn),
+            (A.at[c, u, :, lanes(mz, h)], p_sem.at[1, h], zn),
+            (A.at[c, u, :, lanes(md, h)], dp_sem.at[h], dn),
+        ):
+            remote(ref, ref, send.at[5], sem, to).start()
+
+    def first_arrive(h):
+        for m, sem in ((my, p_sem.at[0, h]), (mz, p_sem.at[1, h]), (md, dp_sem.at[h])):
+            wait_bytes(A.at[c, m, :, lanes(u, h)], sem)
+            x_send(m, h)
+        local(A.at[c, :, :, lanes(u, h)], B.at[x, h], own_sem.at[h]).start()
+
+    def rest_sends():
+        for v0, v1 in ((u, u), (mz, my), (md, md)):
+            remote(panel(u, v0), panel(u, v0), send.at[5], n_sem.at[0, v0], yn).start()
+            remote(panel(u, v1), panel(u, v1), send.at[5], n_sem.at[1, v1], zn).start()
+
+    def pass_on(which, v):
         m = (my, mz)[which]
-        wait_bytes(panel(m, v, h), n_sem.at[which, v, h])
+        half = panel(m, v, pl.ds(which * 128, 128))
+        remote(half, half, send.at[5], d_sem.at[which, v], (zn, yn)[which]).start()
+
+    def n_arrive(which, v, forward):
+        m = (my, mz)[which]
+        wait_bytes(panel(m, v), n_sem.at[which, v])
         if forward:
-            half = A.at[c, m, pl.ds(which * 128, 128), lanes(v, h)]
-            remote(half, half, send.at[5], d_sem.at[which, v, h], (zn, yn)[which]).start()
-        core_send(m, panel(m, v, h))
-
-    def first_arrive(h):
-        n_arrive(0, u, h, True)
-        x_send(my, h)
-        n_arrive(1, u, h, True)
-        x_send(mz, h)
-        wait_bytes(panel(md, u, h), dp_sem.at[h])
-        x_send(md, h)
-        core_send(md, panel(md, u, h))
-        local(A.at[c, :, :, lanes(u, h)], B.at[x, h], own_sem.at[h]).start()
+            pass_on(which, v)
+        core_send(m, panel(m, v))
 
     def x_arrive(m, h, odd):
         wait_bytes(B.at[xl, h, m], x_sem.at[0, h, m])
@@ -243,12 +243,15 @@
         if odd:
             remote(B.at[xr, h, m], B.at[xr, h, m], send.at[4], x_sem.at[2, h, m], left).start()
 
-    def d_arrive(h):
-        for r in (1, 2, 3):
-            v = u ^ r
-            for which in range(2):
-                half = A.at[c, md, pl.ds(which * 128, 128), lanes(v, h)]
-                wait_bytes(half, d_sem.at[which, v, h])
+    def x_far(h):
+        for m in (u, my, mz, md):
+            wait_bytes(B.at[xo, h, m], x_sem.at[2, h, m])
+
+    def d_arrive():
+        for v0, v1 in ((mz, my), (md, md), (my, mz)):
+            for which, v in ((0, v0), (1, v1)):
+                half = panel(md, v, pl.ds(which * 128, 128))
+                wait_bytes(half, d_sem.at[which, v])
                 core_send(md, half)
 
     def regroup(xp, h):
@@ -290,8 +293,8 @@
         to_y = T2.at[pl.ds(uz_ * 4, 4), y, c]
         to_z = T2.at[pl.ds(uy_ * 4, 4), z, c]
         y_done, z_done = ret1.at[uz_, uy], ret1.at[uy_, uz]
-        for d in (1, 3, 2, 0):
-            to = (Y + d) % 4
+        for d in (2, 1, 3, 0):
+            to = (Y + d + (flip // 2) * uy) % 4
             ref = O.at[at * 8 + to]
             if d == 0 and flip // 2 == 0:
 
@@ -304,7 +307,7 @@
                     remote(ref, to_y, send.at[7], y_done, partner).start()
             else:
                 remote(ref, to_y, send.at[7], y_done, dev(x, z, 2 * to + uy_, 0)).start()
-            to = (Z + d) % 4
+            to = (Z + d + (flip % 2) * uz) % 4
             ref2 = O.at[at * 8 + 4 + to]
             if d == 0 and flip % 2 == 0:
 
@@ -323,8 +326,8 @@
         half, parity = b8 // 2, (b8 % 2) ^ flip
         for side in range(2):
             wait_bytes(O.at[pl.ds(0, 8)], ret1.at[parity, side])
-        for d in (1, 3, 2, 0):
-            to = (half + d) % 4
+        for d in (2, 1, 3, 0):
+            to = (half + d + flip * (b8 % 2)) % 4
             ref = T2.at[parity * 4 + to]
             if d == 0 and flip == 0:
                 local(ref, out.at[b8], ret2).start()
@@ -336,62 +339,58 @@
 
     wait_bytes(tbl, tbl_sem)
     transform(0, 0)
+    pl.semaphore_wait(barrier, 15)
+    scatter_y(0)
     transform(0, 1)
-    pl.semaphore_wait(barrier, 32)
-    scatter(0)
+    scatter_z(0)
     transform(1, 0)
+    scatter_y(1)
     transform(1, 1)
-    scatter(1)
+    scatter_z(1)
     wait_bytes(weights, src_sem)
     scatter2(0)
     scatter2(1)
     settle(0)
     first_sends(0)
-    rest_sends(0)
-    first_arrive(0)
     settle(1)
     first_sends(1)
     core_send(u, A.at[c, u])
-    rest_sends(1)
+    rest_sends()
+    first_arrive(0)
     x_arrive(u, 0, False)
-    n_arrive(0, my, 0, True)
-    n_arrive(1, mz, 0, True)
-    x_arrive(my, 0, True)
+    x_arrive(u, 1, True)
     first_arrive(1)
+    pass_on(0, u)
+    pass_on(1, u)
+    for m in (my, mz, md):
+        core_send(m, panel(m, u))
+    x_arrive(my, 0, False)
+    x_arrive(mz, 0, True)
+    x_arrive(md, 0, False)
     wait_bytes(B.at[x, 0], own_sem.at[0])
     regroup(x, 0)
-    n_arrive(0, md, 0, True)
-    n_arrive(1, md, 0, True)
-    x_arrive(mz, 0, False)
-    n_arrive(0, mz, 0, False)
-    n_arrive(1, my, 0, False)
-    x_arrive(md, 0, True)
+    n_arrive(0, my, True)
+    n_arrive(1, mz, True)
     regroup(xl, 0)
     regroup(xr, 0)
-    x_arrive(u, 1, False)
-    n_arrive(0, my, 1, True)
-    n_arrive(1, mz, 1, True)
     x_arrive(my, 1, True)
+    n_arrive(0, md, True)
+    n_arrive(1, md, True)
+    x_arrive(mz, 1, False)
     wait_bytes(B.at[x, 1], own_sem.at[1])
     regroup(x, 1)
-    n_arrive(0, md, 1, True)
-    n_arrive(1, md, 1, True)
-    x_arrive(mz, 1, False)
-    n_arrive(0, mz, 1, False)
-    n_arrive(1, my, 1, False)
     x_arrive(md, 1, True)
+    n_arrive(0, mz, False)
+    n_arrive(1, my, False)
     regroup(xl, 1)
     regroup(xr, 1)
-    d_arrive(0)
-    for m in (u, my, mz, md):
-        wait_bytes(B.at[xo, 0, m], x_sem.at[2, 0, m])
+    x_far(0)
     regroup(xo, 0)
-    for m in (u, my, mz, md):
-        wait_bytes(B.at[xo, 1, m], x_sem.at[2, 1, m])
+    x_far(1)
     regroup(xo, 1)
     multiply(0, 0)
     multiply(1, 2)
-    d_arrive(1)
+    d_arrive()
     multiply(2, 1)
     multiply(3, 3)
     back2(0)
@@ -408,25 +407,32 @@
     wait_bytes(T2.at[pl.ds(0, 7)], send.at[8])
 
 
-def restore_kernel(spectra, table, out, held, sem):
+def restore_kernel(spectra, table, out, held, tbl, result, load_sem, tbl_sem, sem):
     c = lax.axis_index("col") % 2
+    loads = [pltpu.make_async_copy(spectra.at[:, :, core], held.at[core], load_sem.at[core]) for core in range(2)]
+    loads[0].start()
+    load_table = pltpu.make_async_copy(table, tbl, tbl_sem)
+    load_table.start()
+    loads[1].start()
+    load_table.wait()
     copies = []
     for n in range(8):
         core, uy, uz = n // 4, (n // 2) % 2, n % 2
+        if n % 4 == 0:
+            loads[core].wait()
         tiles = []
         for j in range(16):
             y, z = 2 * (j // 4) + uy, 2 * (j % 4) + uz
             b, a = jnp.where(c == 0, z, y), jnp.where(c == 0, y, z)
-            tiles.append(spectra[b, a, core])
-        left = jnp.concatenate(tiles, axis=0)
-        traces = lax.dot_general(left, table[...], (((0,), (0,)), ((), ())), preferred_element_type=F32)
-        traces = traces.astype(BF16)
+            tiles.append(held[core, b, a])
+        tiles = jnp.stack(tiles).astype(F32).reshape(16, 2, 8, 128)
         for h in range(2):
+            left = tiles[:, h].reshape(128, 128).T.astype(BF16)
+            traces = jnp.dot(left, tbl[...], preferred_element_type=F32).astype(BF16)
             for s in range(4):
-                k = (h * 4 + s) * 128
-                held[s, n * 256 + h * 128 : n * 256 + h * 128 + 128, :] = traces[:, k : k + 128]
+                result[s, n * 256 + h * 128 : n * 256 + h * 128 + 128, :] = traces[:, s * 128 : s * 128 + 128]
         rows = pl.ds(n * 256, 256)
-        copy = pltpu.make_async_copy(held.at[:, rows, :], out.at[:, rows, :], sem.at[n])
+        copy = pltpu.make_async_copy(result.at[:, rows, :], out.at[:, rows, :], sem.at[n])
         copy.start()
         copies.append(copy)
     for copy in copies:
@@ -435,14 +441,13 @@
 
 def on_device(forward, backward, traces, source_inverse):
     hbm = pl.BlockSpec(memory_space=pltpu.HBM)
-    vmem = pl.BlockSpec(memory_space=pltpu.VMEM)
     dma = pltpu.SemaphoreType.DMA
     width = traces.shape[1]
     spectra = pl.pallas_call(
         functools.partial(exchange_kernel, 1.0 / math.sqrt(width)),
         out_shape=jax.ShapeDtypeStruct((8, 8, 2, 16, 128), BF16),
         in_specs=[hbm, hbm, hbm],
-        out_specs=vmem,
+        out_specs=hbm,
         scratch_shapes=[
             pltpu.VMEM((2, 4, 4, 2, 128, 128), BF16),
             pltpu.VMEM((128, 512), BF16),
@@ -464,9 +469,10 @@
             dma(()),
             dma((9,)),
             dma((3, 2, 4)),
-            dma((2, 4, 2)),
+            dma((2, 2)),
+            dma((2, 4)),
             dma((2,)),
-            dma((2, 4, 2)),
+            dma((2, 4)),
             dma((4,)),
             dma((2,)),
         ],
@@ -478,9 +484,16 @@
     return pl.pallas_call(
         restore_kernel,
         out_shape=jax.ShapeDtypeStruct(traces.shape, BF16),
-        in_specs=[vmem, vmem],
+        in_specs=[hbm, hbm],
         out_specs=hbm,
-        scratch_shapes=[pltpu.VMEM((4, width, 128), BF16), dma((8,))],
+        scratch_shapes=[
+            pltpu.VMEM((2, 8, 8, 16, 128), BF16),
+            pltpu.VMEM((128, 512), BF16),
+            pltpu.VMEM((4, width, 128), BF16),
+            dma((2,)),
+            dma(()),
+            dma((8,)),
+        ],
         compiler_params=pltpu.CompilerParams(vmem_limit_bytes=VMEM_LIMIT),
         name="restore",
     )(spectra, jnp.asarray(backward))

time: 72.6 us -> 69 us (0.950)
  Pallas kernels: 72.5 us -> 68.9 us
    pallas_call x1, Pallas kernels: 69.6 us -> 66.1 us  [on_device(): pl.pallas_call(functools.partial(exchange_kernel, 1.0 / math.sqrt(width))...]
where the time goes in v3:
time: 69 us; the launch traced here: 68.9 us
  Pallas kernels  68.9 us (100%)
    pallas_call x1, Pallas kernels, on_device(): pl.pallas_call(functools.partial(exchange_kernel, 1.0 / math.sqrt(width))...  66.1 us
    pallas_call x1, Pallas kernels, on_device(): pl.pallas_call(restore_kernel, out_shape=jax.ShapeDtypeStruct(traces.shap...  2.81 us

profile of v3, /device:TPU:1, one launch (start us, length us, event | category | flops | bytes accessed | tf_op | source)
XLA Modules:
  0.0 68.9 jit_solution(7081669093117918112)
XLA Ops:
  0.0 66.1 %exchange.1.spectra = bf16[8,8,2,16,128]{4,3,2,1,0:T(8,128)(2,1)} custom-call(bf16[4,8,2,128,128]{4,3,2,1,0:T(8,128)(2,1)} %bitcast.1, bf16[128,512]{1,0:T(8,128)(2,1)} %constant.4.clone.table, f32[2,16]{1,0:T(2,128)} %source.1), custom_call_target="tpu_custom_call" | custom-call | tf_op jit(solution)/shard_map/exchange/pallas_call | solution.py:446
  66.1 2.8 %restore.1 = bf16[4,2048,128]{2,1,0:T(8,128)(2,1)} custom-call(bf16[8,8,2,16,128]{4,3,2,1,0:T(8,128)(2,1)} %exchange.1.spectra, bf16[128,512]{1,0:T(8,128)(2,1)} %constant.5.clone.table), custom_call_target="tpu_custom_call" | custom-call | tf_op jit(solution)/shard_map/restore/pallas_call | solution.py:484

commit v4 on v3

v4 whole, which is shorter than its diff:
```python
import functools
import math

import jax
import jax.numpy as jnp
import numpy as np
from jax import lax
from jax.experimental import pallas as pl
from jax.experimental.pallas import tpu as pltpu
from jax.sharding import PartitionSpec as P

MESH = pl.DeviceIdType.MESH
BF16 = jnp.bfloat16
F32 = jnp.float32
VMEM_LIMIT = 62 * 1024 * 1024 + 512 * 1024


def tables(count, length):
    bins = np.arange(count, dtype=np.int32) + 1
    times = np.arange(length, dtype=np.int32)
    index = bins[:, None] * times[None, :] % length
    angle = index.astype(np.float32) * np.float32(2.0 * math.pi / length)
    norm = np.float32(1.0 / math.sqrt(length))
    stacked = np.stack([np.cos(angle), -np.sin(angle)])
    forward = np.zeros((count, 2, 4, 4, length), np.float32)
    for i in range(4):
        forward[:, :, i, i] = np.transpose(stacked * norm, (1, 0, 2))
    forward = forward.reshape(count * 8, 4 * length)
    return forward.astype(jnp.bfloat16), (2 * forward).astype(jnp.bfloat16)


def low_rows(shape):
    return lax.broadcasted_iota(jnp.int32, shape, len(shape) - 2) < 4


def interleave(first, second):
    axis = first.ndim - 2
    low = low_rows(first.shape)
    top = jnp.where(low, first, pltpu.roll(second, 4, axis))
    bottom = jnp.where(low, pltpu.roll(first, 4, axis), second)
    return top, bottom


def exchange_kernel(
    scale,
    traces,
    table,
    source,
    out,
    tr,
    tbl,
    weights,
    S,
    T,
    R,
    A,
    B,
    W,
    acc,
    O,
    T2,
    tr_sem,
    tbl_sem,
    src_sem,
    in1,
    in2,
    ret1,
    ret2,
    send,
    x_sem,
    p_sem,
    n_sem,
    dp_sem,
    d_sem,
    core_sem,
    own_sem,
):
    x = lax.axis_index("freq")
    z = lax.axis_index("row")
    col = lax.axis_index("col")
    y = col // 2
    c = col % 2
    uy, uz = y % 2, z % 2
    Y, Z = y // 2, z // 2
    u = uy * 2 + uz

    def dev(xx, zz, yy, cc):
        return (xx, zz, yy * 2 + cc)

    def remote(src, dst, s, r, to):
        return pltpu.make_async_remote_copy(
            src_ref=src, dst_ref=dst, send_sem=s, recv_sem=r, device_id=to, device_id_type=MESH
        )

    def local(src, dst, s):
        return pltpu.make_async_copy(src, dst, s)

    def wait_bytes(ref, sem):
        pltpu.make_async_copy(ref, ref, sem).wait()

    near = uy

    def part(q):
        return q % 2, near if q < 2 else 1 - near

    def load(q):
        h, w = part(q)
        for core in range(2):
            k = core * 2 + w
            local(traces.at[:, pl.ds(2 * k, 2), h], tr.at[h, k], tr_sem.at[h, k]).start()

    barrier = pltpu.get_barrier_semaphore()
    partner = dev(x, z, y, 1 - c)
    left = dev((x + 3) % 4, z, y, c)
    right = dev((x + 1) % 4, z, y, c)
    yn = dev(x, z, y + 1 - 2 * uy, c)
    zn = dev(x, z + 1 - 2 * uz, y, c)
    dn = dev(x, z + 1 - 2 * uz, y + 1 - 2 * uy, c)
    others = []
    for d in (4, 2, 6):
        a_y, a_z = jnp.where(c == 0, (y + d) % 8, y), jnp.where(c == 0, z, (z + d) % 8)
        b_y, b_z = jnp.where(c == 0, y, (y + d) % 8), jnp.where(c == 0, (z + d) % 8, z)
        others += [dev(x, a_z, a_y, 0), dev(x, a_z, a_y, 1), dev(x, b_z, b_y, c)]
    others += [dn, left, right, yn, zn, partner]
    local(table, tbl, tbl_sem).start()
    load(0)
    for other in others:
        pl.semaphore_signal(barrier, inc=1, device_id=other, device_id_type=MESH)
    for q in range(1, 4):
        load(q)
    local(source, weights, src_sem).start()

    def transform(q, core):
        h, w = part(q)
        k = core * 2 + w
        wait_bytes(tr.at[h, k], tr_sem.at[h, k])
        block = jnp.concatenate([tr[h, k, s].reshape(256, 128) for s in range(4)], axis=1)
        data = lax.dot_general(tbl[...], block, (((1,), (1,)), ((), ())), preferred_element_type=F32)
        data = data.reshape(16, 8, 256)
        data = jnp.concatenate([data[:, :, :128], data[:, :, 128:]], axis=1)
        data = data.astype(BF16).reshape(4, 4, 16, 128)
        for first in range(4):
            if core == 0:
                S[q, first] = data[first]
            else:
                S[q, 4:8, first] = data[first]

    def scatter_y(q):
        for d in (2, 1, 3):
            to = (Y + d) % 4
            remote(S.at[q, to], T.at[q, :, Y, c], send.at[q], in1.at[q], dev(x, z, 2 * to + uy, 0)).start()

        @pl.when(c == 0)
        def _():
            local(S.at[q, Y], T.at[q, :, Y, c], in1.at[q]).start()

        @pl.when(c == 1)
        def _():
            remote(S.at[q, Y], T.at[q, :, Y, c], send.at[q], in1.at[q], partner).start()

    def scatter_z(q):
        for d in (2, 1, 3):
            to = (Z + d) % 4
            remote(S.at[q, 4 + to], T.at[q, :, Z, c], send.at[q], in1.at[q], dev(x, 2 * to + uz, y, 1)).start()

        @pl.when(c == 0)
        def _():
            remote(S.at[q, 4 + Z], T.at[q, :, Z, c], send.at[q], in1.at[q], partner).start()

        @pl.when(c == 1)
        def _():
            local(S.at[q, 4 + Z], T.at[q, :, Z, c], in1.at[q]).start()

    def scatter2(q):
        wait_bytes(T.at[q], in1.at[q])
        b4 = jnp.where(c == 0, Z, Y)
        for d in (2, 1, 3):
            to = (b4 + d) % 4
            far = 2 * to + jnp.where(c == 0, uz, uy)
            yy = jnp.where(c == 0, y, far)
            zz = jnp.where(c == 0, far, z)
            remote(T.at[q, to], R.at[q, b4], send.at[4 + q], in2.at[q], dev(x, zz, yy, c)).start()
        local(T.at[q, b4], R.at[q, b4], in2.at[q]).start()

    def settle(q):
        wait_bytes(R.at[q], in2.at[q])
        h, w = part(q)

        def step(n, carry):
            b, a = n // 4, n % 4
            row = pl.multiple_of(jnp.where(c == 0, a * 4 + b, n) * 16, 16)
            first = R[q, b, a, 0].astype(F32).reshape(2, 8, 128)
            second = R[q, b, a, 1].astype(F32).reshape(2, 8, 128)
            real, imag = interleave(first, second)
            for v in range(2):
                tile = jnp.concatenate([real[v], imag[v]], axis=0).astype(BF16)
                A[c, u, pl.ds(row, 16), pl.ds(pl.multiple_of((2 * w + v) * 256 + h * 128, 128), 128)] = tile
            return carry

        lax.fori_loop(0, 16, step, 0, unroll=4)

    my, mz, md = u ^ 2, u ^ 1, u ^ 3
    xl, xr, xo = (x + 3) % 4, (x + 1) % 4, (x + 2) % 4

    def lanes(v, h):
        return pl.ds(pl.multiple_of(v * 256 + h * 128, 128), 128)

    def panel(m, v, rows=pl.ds(0, 256)):
        return A.at[c, m, rows, pl.ds(pl.multiple_of(v * 256, 256), 256)]

    def x_send(m, h):
        ref = A.at[c, m, :, lanes(u, h)]
        remote(ref, B.at[x, h, m], send.at[8], x_sem.at[0, h, m], right).start()
        remote(ref, B.at[x, h, m], send.at[8], x_sem.at[1, h, m], left).start()

    def core_send(m, ref):
        remote(ref, ref, send.at[10], core_sem.at[m], partner).start()

    def first_send(which, h):
        v, sem, to = ((my, p_sem.at[0, h], yn), (mz, p_sem.at[1, h], zn), (md, dp_sem.at[h], dn))[which]
        ref = A.at[c, u, :, lanes(v, h)]
        remote(ref, ref, send.at[9], sem, to).start()

    def first_arrive(which, h):
        m, sem = ((my, p_sem.at[0, h]), (mz, p_sem.at[1, h]), (md, dp_sem.at[h]))[which]
        wait_bytes(A.at[c, m, :, lanes(u, h)], sem)
        x_send(m, h)

    def own_copy(h):
        return local(A.at[c, :, :, lanes(u, h)], B.at[x, h], own_sem.at[h])

    def rest_sends():
        for v0, v1 in ((u, u), (mz, my), (md, md)):
            remote(panel(u, v0), panel(u, v0), send.at[9], n_sem.at[0, v0], yn).start()
            remote(panel(u, v1), panel(u, v1), send.at[9], n_sem.at[1, v1], zn).start()

    def pass_on(which, v):
        m = (my, mz)[which]
        half = panel(m, v, pl.ds(which * 128, 128))
        remote(half, half, send.at[9], d_sem.at[which, v], (zn, yn)[which]).start()

    def n_arrive(which, v, forward):
        m = (my, mz)[which]
        wait_bytes(panel(m, v), n_sem.at[which, v])
        if forward:
            pass_on(which, v)
        core_send(m, panel(m, v))

    def x_arrive(m, h, odd):
        wait_bytes(B.at[xl, h, m], x_sem.at[0, h, m])
        if not odd:
            remote(B.at[xl, h, m], B.at[xl, h, m], send.at[8], x_sem.at[2, h, m], right).start()
        wait_bytes(B.at[xr, h, m], x_sem.at[1, h, m])
        if odd:
            remote(B.at[xr, h, m], B.at[xr, h, m], send.at[8], x_sem.at[2, h, m], left).start()

    def x_far(h):
        for m in (u, my, mz, md):
            wait_bytes(B.at[xo, h, m], x_sem.at[2, h, m])

    def d_arrive():
        for v0, v1 in ((mz, my), (md, md), (my, mz)):
            for which, v in ((0, v0), (1, v1)):
                half = panel(md, v, pl.ds(which * 128, 128))
                wait_bytes(half, d_sem.at[which, v])
                core_send(md, half)

    def regroup(xp, h):
        def step(n, carry):
            uz_, Z_, Y_ = n // 16, (n // 4) % 4, n % 4
            row = pl.multiple_of((Y_ * 4 + Z_) * 16, 16)
            even = B[xp, h, uz_, pl.ds(row, 16), :].astype(F32)
            odd = B[xp, h, 2 + uz_, pl.ds(row, 16), :].astype(F32)
            at = pl.ds(pl.multiple_of((2 * Z_ + uz_) * 64 + Y_ * 16, 16), 16)
            W[xp, at, h * 128 : h * 128 + 128] = jnp.concatenate([even[:8], odd[:8]], axis=0).astype(BF16)
            W[xp, at, 256 + h * 128 : 384 + h * 128] = jnp.concatenate([even[8:], odd[8:]], axis=0).astype(BF16)
            return carry

        lax.fori_loop(0, 32, step, 0, unroll=8)

    j = Y * 4 + Z

    def term(m, xp):
        left = A[xp // 2, m, :, pl.ds(pl.multiple_of((xp % 2) * 512, 512), 512)]
        return jnp.dot(left, W[xp], preferred_element_type=F32)

    def multiply(at, flip):
        m = u ^ flip
        w_real, w_imag = weights[0, j], weights[1, j]
        if flip == 0:
            total = acc[...] + term(m, xo)
        else:
            wait_bytes(A.at[1 - c, m], core_sem.at[m])
            total = jnp.dot(A[0, m], W[0:2].reshape(1024, 512), preferred_element_type=F32)
            total += jnp.dot(A[1, m], W[2:4].reshape(1024, 512), preferred_element_type=F32)
        total = total.reshape(16, 2, 8, 512)
        real = total[:, 0, :, :256] - total[:, 1, :, 256:]
        imag = total[:, 0, :, 256:] + total[:, 1, :, :256]
        pred_real = (w_real * real - w_imag * imag) * scale
        pred_imag = (w_real * imag + w_imag * real) * scale
        for core, part in enumerate(interleave(pred_real, pred_imag)):
            part = jnp.concatenate([part[:, :, :128], part[:, :, 128:]], axis=1).astype(BF16)
            part = part.reshape(4, 4, 16, 128)
            for first in range(4):
                if core == 0:
                    O[at * 8 + first] = part[first]
                else:
                    O[at * 8 + 4 : at * 8 + 8, first] = part[first]

        uy_, uz_ = uy ^ (flip // 2), uz ^ (flip % 2)
        to_y = T2.at[pl.ds(uz_ * 4, 4), uy, Y, c]
        to_z = T2.at[pl.ds(uy_ * 4, 4), uz, Z, c]
        y_done, z_done = ret1.at[uz_, uy], ret1.at[uy_, uz]
        for d in (2, 1, 3, 0):
            to = (Y + d + (flip // 2) * uy) % 4
            ref = O.at[at * 8 + to]
            if d == 0 and flip // 2 == 0:

                @pl.when(c == 0)
                def _():
                    local(ref, to_y, y_done).start()

                @pl.when(c == 1)
                def _():
                    remote(ref, to_y, send.at[11], y_done, partner).start()
            else:
                remote(ref, to_y, send.at[11], y_done, dev(x, z, 2 * to + uy_, 0)).start()
            to = (Z + d + (flip % 2) * uz) % 4
            ref2 = O.at[at * 8 + 4 + to]
            if d == 0 and flip % 2 == 0:

                @pl.when(c == 1)
                def _():
                    local(ref2, to_z, z_done).start()

                @pl.when(c == 0)
                def _():
                    remote(ref2, to_z, send.at[11], z_done, partner).start()
            else:
                remote(ref2, to_z, send.at[11], z_done, dev(x, 2 * to + uz_, y, 1)).start()

    def back2(flip):
        b8, own = jnp.where(c == 0, z, y), jnp.where(c == 0, uz, uy)
        differ = jnp.where(c == 0, flip % 2, flip // 2)
        parity = own ^ differ
        side = jnp.where(c == 0, uy ^ (flip // 2), uz ^ (flip % 2))
        wait_bytes(O.at[pl.ds(0, 8)], ret1.at[parity, side])
        for d in (2, 1, 3, 0):
            to = (b8 // 2 + d + differ * own) % 4
            ref = T2.at[parity * 4 + to, side]
            far = 2 * to + parity
            yy = jnp.where(c == 0, y, far)
            zz = jnp.where(c == 0, far, z)
            if d == 0 and flip != 3:

                @pl.when(differ == 0)
                def _():
                    local(ref, out.at[b8, side], ret2).start()

                @pl.when(differ != 0)
                def _():
                    remote(ref, out.at[b8, side], send.at[12], ret2, dev(x, zz, yy, c)).start()
            else:
                remote(ref, out.at[b8, side], send.at[12], ret2, dev(x, zz, yy, c)).start()

    wait_bytes(tbl, tbl_sem)
    for q in range(4):
        transform(q, 0)
        if q == 0:
            pl.semaphore_wait(barrier, 15)
        scatter_y(q)
        transform(q, 1)
        scatter_z(q)
    wait_bytes(weights, src_sem)
    for q in range(4):
        scatter2(q)
    settle(0)
    x_send(u, 0)
    first_send(1, 0)
    settle(1)
    x_send(u, 1)
    first_send(1, 1)
    settle(2)
    first_send(0, 0)
    first_send(2, 0)
    settle(3)
    first_send(0, 1)
    first_send(2, 1)
    core_send(u, A.at[c, u])
    rest_sends()
    first_arrive(1, 0)
    first_arrive(1, 1)
    x_arrive(u, 0, False)
    x_arrive(u, 1, True)
    pass_on(1, u)
    first_arrive(0, 0)
    first_arrive(2, 0)
    own_copy(0).start()
    first_arrive(0, 1)
    first_arrive(2, 1)
    own_copy(1).start()
    pass_on(0, u)
    for m in (my, mz, md):
        core_send(m, panel(m, u))
    x_arrive(mz, 0, False)
    x_arrive(mz, 1, True)
    x_arrive(my, 0, False)
    x_arrive(md, 0, True)
    wait_bytes(B.at[x, 0], own_sem.at[0])
    regroup(x, 0)
    n_arrive(0, my, True)
    n_arrive(1, mz, True)
    regroup(xl, 0)
    regroup(xr, 0)
    x_arrive(my, 1, False)
    n_arrive(0, md, True)
    n_arrive(1, md, True)
    x_arrive(md, 1, True)
    wait_bytes(B.at[x, 1], own_sem.at[1])
    regroup(x, 1)
    n_arrive(0, mz, False)
    n_arrive(1, my, False)
    regroup(xl, 1)
    regroup(xr, 1)
    wait_bytes(A.at[1 - c, u], core_sem.at[u])
    acc[...] = term(u, x)
    acc[...] += term(u, xl)
    acc[...] += term(u, xr)
    x_far(0)
    regroup(xo, 0)
    x_far(1)
    regroup(xo, 1)
    multiply(0, 0)
    multiply(1, 2)
    d_arrive()
    multiply(2, 1)
    multiply(3, 3)
    for flip in (0, 2, 1, 3):
        back2(flip)
    wait_bytes(out, ret2)

    for q in range(4):
        wait_bytes(S.at[q, pl.ds(0, 7)], send.at[q])
        wait_bytes(T.at[q, pl.ds(0, 3)], send.at[4 + q])
    wait_bytes(B.at[pl.ds(0, 3)], send.at[8])
    wait_bytes(A.at[0, pl.ds(0, 3)], send.at[9])
    wait_bytes(A.at[0], send.at[10])
    wait_bytes(O.at[pl.ds(0, 30)], send.at[11])
    wait_bytes(T2.at[pl.ds(0, 7)], send.at[12])


def restore_kernel(spectra, table, out, held, tbl, result, load_sem, tbl_sem, sem):
    c = lax.axis_index("col") % 2
    loads = [pltpu.make_async_copy(spectra.at[:, :, :, core], held.at[core], load_sem.at[core]) for core in range(2)]
    loads[0].start()
    load_table = pltpu.make_async_copy(table, tbl, tbl_sem)
    load_table.start()
    loads[1].start()
    load_table.wait()
    copies = []
    for n in range(8):
        core, uy, uz = n // 4, (n // 2) % 2, n % 2
        if n % 4 == 0:
            loads[core].wait()
        tiles = []
        for j in range(16):
            y, z = 2 * (j // 4) + uy, 2 * (j % 4) + uz
            b, a = jnp.where(c == 0, z, y), jnp.where(c == 0, y, z)
            tiles.append(held[core, b, a % 2, a // 2])
        tiles = jnp.stack(tiles).astype(F32).reshape(16, 2, 8, 128)
        for h in range(2):
            left = tiles[:, h].reshape(128, 128).T.astype(BF16)
            traces = jnp.dot(left, tbl[...], preferred_element_type=F32).astype(BF16)
            for s in range(4):
                result[s, n * 256 + h * 128 : n * 256 + h * 128 + 128, :] = traces[:, s * 128 : s * 128 + 128]
        rows = pl.ds(n * 256, 256)
        copy = pltpu.make_async_copy(result.at[:, rows, :], out.at[:, rows, :], sem.at[n])
        copy.start()
        copies.append(copy)
    for copy in copies:
        copy.wait()


def on_device(forward, backward, traces, source_inverse):
    hbm = pl.BlockSpec(memory_space=pltpu.HBM)
    dma = pltpu.SemaphoreType.DMA
    width = traces.shape[1]
    spectra = pl.pallas_call(
        functools.partial(exchange_kernel, 1.0 / math.sqrt(width)),
        out_shape=jax.ShapeDtypeStruct((8, 2, 4, 2, 16, 128), BF16),
        in_specs=[hbm, hbm, hbm],
        out_specs=hbm,
        scratch_shapes=[
            pltpu.VMEM((2, 4, 4, 2, 128, 128), BF16),
            pltpu.VMEM((128, 512), BF16),
            pltpu.SMEM((2, 16), F32),
            pltpu.VMEM((4, 8, 4, 16, 128), BF16),
            pltpu.VMEM((4, 4, 4, 2, 16, 128), BF16),
            pltpu.VMEM((4, 4, 4, 2, 16, 128), BF16),
            pltpu.VMEM((2, 4, 256, 1024), BF16),
            pltpu.VMEM((4, 2, 4, 256, 128), BF16),
            pltpu.VMEM((4, 512, 512), BF16),
            pltpu.VMEM((256, 512), F32),
            pltpu.VMEM((32, 4, 16, 128), BF16),
            pltpu.VMEM((8, 2, 4, 2, 16, 128), BF16),
            dma((2, 4)),
            dma(()),
            dma(()),
            dma((4,)),
            dma((4,)),
            dma((2, 2)),
            dma(()),
            dma((13,)),
            dma((3, 2, 4)),
            dma((2, 2)),
            dma((2, 4)),
            dma((2,)),
            dma((2, 4)),
            dma((4,)),
            dma((2,)),
        ],
        compiler_params=pltpu.CompilerParams(
            collective_id=0, has_side_effects=True, vmem_limit_bytes=VMEM_LIMIT
        ),
        name="exchange",
    )(traces.reshape(4, 8, 2, 128, 128), jnp.asarray(forward), source_inverse)
    return pl.pallas_call(
        restore_kernel,
        out_shape=jax.ShapeDtypeStruct(traces.shape, BF16),
        in_specs=[hbm, hbm],
        out_specs=hbm,
        scratch_shapes=[
            pltpu.VMEM((2, 8, 2, 4, 16, 128), BF16),
            pltpu.VMEM((128, 512), BF16),
            pltpu.VMEM((4, width, 128), BF16),
            dma((2,)),
            dma(()),
            dma((8,)),
        ],
        compiler_params=pltpu.CompilerParams(vmem_limit_bytes=VMEM_LIMIT),
        name="restore",
    )(spectra, jnp.asarray(backward))


def solution(mesh):
    forward, backward = tables(16, 128)
    in_specs = (P(("freq", "row", "col"), None, None), P())
    out_specs = P(("freq", "row", "col"), None, None)
    return jax.shard_map(
        functools.partial(on_device, forward, backward),
        mesh=mesh,
        in_specs=in_specs,
        out_specs=out_specs,
        check_vma=False,
    )
```

time: 69 us -> 66.1 us (0.958)
  Pallas kernels: 68.9 us -> 66 us
    pallas_call x1, Pallas kernels: 66.1 us -> 63 us  [on_device(): pl.pallas_call(functools.partial(exchange_kernel, 1.0 / math.sqrt(width))...]
where the time goes in v4:
time: 66.1 us; the launch traced here: 66 us
  Pallas kernels  66 us (100%)
    pallas_call x1, Pallas kernels, on_device(): pl.pallas_call(functools.partial(exchange_kernel, 1.0 / math.sqrt(width))...  63 us
    pallas_call x1, Pallas kernels, on_device(): pl.pallas_call(restore_kernel, out_shape=jax.ShapeDtypeStruct(traces.shap...  3.01 us

profile of v4, /device:TPU:1, one launch (start us, length us, event | category | flops | bytes accessed | tf_op | source)
XLA Modules:
  0.0 66.0 jit_solution(42298200164182537)
XLA Ops:
  0.0 63.0 %exchange.1.spectra = bf16[8,2,4,2,16,128]{5,4,3,2,1,0:T(8,128)(2,1)} custom-call(bf16[4,8,2,128,128]{4,3,2,1,0:T(8,128)(2,1)} %bitcast.1, bf16[128,512]{1,0:T(8,128)(2,1)} %constant.4.clone.table, f32[2,16]{1,0:T(2,128)} %source.1), custom_call_target="tpu_custom_call" | custom-call | tf_op jit(solution)/shard_map/exchange/pallas_call | solution.py:488
  63.0 3.0 %restore.1 = bf16[4,2048,128]{2,1,0:T(8,128)(2,1)} custom-call(bf16[8,2,4,2,16,128]{5,4,3,2,1,0:T(8,128)(2,1)} %exchange.1.spectra, bf16[128,512]{1,0:T(8,128)(2,1)} %constant.5.clone.table), custom_call_target="tpu_custom_call" | custom-call | tf_op jit(solution)/shard_map/restore/pallas_call | solution.py:527

commit v5 on v4

--- a/solution.py
+++ b/solution.py
@@ -253,6 +253,12 @@
         wait_bytes(B.at[xr, h, m], x_sem.at[1, h, m])
         if odd:
             remote(B.at[xr, h, m], B.at[xr, h, m], send.at[8], x_sem.at[2, h, m], left).start()
+
+    def x_arrive_last(m, h):
+        for side, (src, to) in enumerate(((xl, right), (xr, left))):
+            wait_bytes(B.at[src, h, m], x_sem.at[side, h, m])
+            half = B.at[src, h, m, pl.ds(side * 128, 128), :]
+            remote(half, half, send.at[8], x_sem.at[2, h, m], to).start()
 
     def x_far(h):
         for m in (u, my, mz, md):
@@ -410,12 +416,12 @@
     regroup(x, 0)
     n_arrive(0, my, True)
     n_arrive(1, mz, True)
+    x_arrive_last(my, 1)
+    n_arrive(0, md, True)
+    n_arrive(1, md, True)
+    x_arrive_last(md, 1)
     regroup(xl, 0)
     regroup(xr, 0)
-    x_arrive(my, 1, False)
-    n_arrive(0, md, True)
-    n_arrive(1, md, True)
-    x_arrive(md, 1, True)
     wait_bytes(B.at[x, 1], own_sem.at[1])
     regroup(x, 1)
     n_arrive(0, mz, False)

time: 66.1 us -> 66.3 us (level)
  no operation moved by 1% of the time
where the time goes in v5:
time: 66.3 us; the launch traced here: 66.1 us
  Pallas kernels  66.1 us (100%)
    pallas_call x1, Pallas kernels, on_device(): pl.pallas_call(functools.partial(exchange_kernel, 1.0 / math.sqrt(width))...  63.1 us
    pallas_call x1, Pallas kernels, on_device(): pl.pallas_call(restore_kernel, out_shape=jax.ShapeDtypeStruct(traces.shap...  3.01 us

profile of v5, /device:TPU:1, one launch (start us, length us, event | category | flops | bytes accessed | tf_op | source)
XLA Modules:
  0.0 66.1 jit_solution(6107699681089152488)
XLA Ops:
  0.0 63.1 %exchange.1.spectra = bf16[8,2,4,2,16,128]{5,4,3,2,1,0:T(8,128)(2,1)} custom-call(bf16[4,8,2,128,128]{4,3,2,1,0:T(8,128)(2,1)} %bitcast.1, bf16[128,512]{1,0:T(8,128)(2,1)} %constant.4.clone.table, f32[2,16]{1,0:T(2,128)} %source.1), custom_call_target="tpu_custom_call" | custom-call | tf_op jit(solution)/shard_map/exchange/pallas_call | solution.py:494
  63.1 3.0 %restore.1 = bf16[4,2048,128]{2,1,0:T(8,128)(2,1)} custom-call(bf16[8,2,4,2,16,128]{5,4,3,2,1,0:T(8,128)(2,1)} %exchange.1.spectra, bf16[128,512]{1,0:T(8,128)(2,1)} %constant.5.clone.table), custom_call_target="tpu_custom_call" | custom-call | tf_op jit(solution)/shard_map/restore/pallas_call | solution.py:533
